TPU v7x, 32 devices: a whole 2x2x4 slice. The times are simulated.
32 devices in a mesh: groups: 2 (over y), dp: 4 (over z), feat: 2 (over x), sub: 2 (over core).
Axes of the slice: x: 2, y: 2, z: 4, core: 2. Of those that a mesh axis runs over, the one named last changes fastest.
Arguments:
- bins: int32 [32768, 1024], P(('groups', 'dp', 'sub'), 'feat'), parts along dimension 0, may hold values from 0 to 127
- grads: bfloat16 [32768, 32], P(('groups', 'dp', 'sub')), parts along dimension 0, may hold values from -6 to 6
- hess: bfloat16 [32768], P(('groups', 'dp', 'sub')), parts along dimension 0, may hold values from 0.25 to 4
- node_side: int32 [32768], P(('groups', 'dp', 'sub')), parts along dimension 0, may hold values from 0 to 1
- signs: int32 [2048], P('groups'), parts along dimension 0, may hold values from -1 to 1
- child_owner: int32 [16], P('groups'), parts along dimension 0, may hold values from 0 to 7, each once
- parent_owner: int32 [16], P('groups'), parts along dimension 0, may hold values from 0 to 7, each once
- parent_grad: float32 [16, 128, 4096], P(('groups', 'dp', 'sub'), 'feat'), parts along dimension 0, may hold values from -48 to 48
- parent_hess: float32 [16, 128, 128], P(('groups', 'dp', 'sub'), 'feat'), parts along dimension 0, may hold values from 33 to 516
- node_low: int32 [4], P('groups'), parts along dimension 0, may hold values from -40 to -5
- node_high: int32 [4], P('groups'), parts along dimension 0, may hold values from 5 to 40
Outputs:
- gains: float32 [16, 128, 2, 128], P(('groups', 'dp', 'sub'), 'feat'), parts along dimension 0
There are 2 independent parts, one for each index of `groups`. A program takes and returns all parts, laid end to end along the dimension named above; each array names one. Nothing has to cross between parts.
Inputs may be any that keep to these rules, and one draw needn't show every extreme that they name: `child_owner`: each slot number appears once. `parent_owner`: each slot number appears once.
All inputs are finite; a program needn't handle non-finite values.
Results may differ from a plain program's by a relative error of at most 0.0003.
Values sent between devices are 32-bit elements; how exact they have to be, the bound alone decides.
No kernel may reach another device: no remote copies, remote signals or barrier semaphores. Data moves between devices by JAX's collectives and lax.ppermute only.
A program may use at most 128 MiB of HBM per device.

v0:
```python
import jax
import jax.numpy as jnp
from jax import lax
from jax.sharding import PartitionSpec as P

reg_lambda = 1.0


def side_score(grad_sum, hess_sum, low, high):
    denom = jnp.maximum(hess_sum, 0.0) + reg_lambda
    weight = jnp.clip(-grad_sum / denom[..., None], low[..., None], high[..., None])
    return -jnp.mean(2.0 * grad_sum * weight + denom[..., None] * weight * weight, axis=-1)


def split_gains(grad_hist, hess_hist, sign_vec, low, high):
    left_grad = jnp.cumsum(grad_hist, axis=1)
    left_hess = jnp.cumsum(hess_hist, axis=1)
    right_grad = left_grad[:, -1:, :] - left_grad
    right_hess = left_hess[:, -1:] - left_hess
    middle = 0.5 * (low + high)
    sign_col = sign_vec[:, None]
    ones_like = jnp.ones_like(left_hess)
    low_left = jnp.where(sign_col < 0, middle, low) * ones_like
    high_left = jnp.where(sign_col > 0, middle, high) * ones_like
    low_right = jnp.where(sign_col > 0, middle, low) * ones_like
    high_right = jnp.where(sign_col < 0, middle, high) * ones_like
    return side_score(left_grad, left_hess, low_left, high_left) + side_score(
        right_grad, right_hess, low_right, high_right
    )


def inverse_of(owner, slots):
    return jnp.sum(jnp.where(owner[None, :] == slots[:, None], slots[None, :], 0), axis=1)


def choose_piece(source, carry, pieces):
    first = jax.tree.leaves(pieces)[0]
    index = jnp.arange(first.shape[0], dtype=jnp.int32)
    hit = index == source

    def add_one(total, piece):
        mask = hit.reshape((-1,) + (1,) * (piece.ndim - 1))
        return jnp.sum(jnp.where(mask, piece, jnp.float32(0.0)), axis=0)

    return jax.tree.map(add_one, carry, pieces)


def per_device(
    bins,
    grads,
    hess,
    node_side,
    signs,
    child_owner,
    parent_owner,
    parent_grad,
    parent_hess,
    node_low,
    node_high,
):
    owners = lax.axis_size(("dp", "sub"))
    place = lax.axis_index(("dp", "sub"))
    column = lax.axis_index("feat")
    rows, f_dev = bins.shape
    kdim = grads.shape[1]
    nbins = parent_hess.shape[2]
    slab = parent_grad.shape[1]
    slots = jnp.arange(owners, dtype=jnp.int32)
    child_inv = inverse_of(child_owner, slots)
    child_slab = child_inv[place]
    source = parent_owner[child_slab]
    inside = node_side == 1
    stacked = jnp.concatenate([grads, hess[:, None]], axis=1)
    weighted = jnp.transpose(jnp.where(inside[:, None], stacked, jnp.zeros_like(stacked)))
    ordered = jnp.take(bins.reshape(rows, owners, slab), child_inv, axis=1)
    blocks = jnp.transpose(ordered.reshape(rows, f_dev).reshape(rows, f_dev // 16, 16), (1, 0, 2))
    levels = jnp.arange(nbins, dtype=jnp.int32)

    def block_sums(block):
        onehot = (block[:, :, None] == levels).astype(jnp.bfloat16).reshape(rows, 16 * nbins)
        return jnp.dot(weighted, onehot, preferred_element_type=jnp.float32)

    sums = lax.map(block_sums, blocks).reshape(f_dev // 16, kdim + 1, 16, nbins)
    sums = jnp.transpose(sums, (0, 2, 3, 1)).reshape(owners, slab, nbins, kdim + 1)
    term_grad = sums[..., :kdim].reshape(owners, slab, nbins * kdim)
    term_hess = sums[..., kdim]
    summed = (
        lax.psum_scatter(term_grad, ("dp", "sub"), scatter_dimension=0, tiled=True),
        lax.psum_scatter(term_hess, ("dp", "sub"), scatter_dimension=0, tiled=True),
    )
    small_grad = summed[0].reshape(slab, nbins, kdim)
    small_hess = summed[1].reshape(slab, nbins)
    low = node_low.astype(jnp.float32) / 1024.0
    high = node_high.astype(jnp.float32) / 1024.0
    feature_ids = column * f_dev + child_slab * slab + jnp.arange(slab, dtype=jnp.int32)
    sign_vec = jnp.take(signs, feature_ids)
    empty = (jnp.zeros((slab, nbins * kdim), jnp.float32), jnp.zeros((slab, nbins), jnp.float32))
    par_grad, par_hess = choose_piece(
        source,
        empty,
        (
            lax.all_gather(parent_grad, ("dp", "sub"), axis=0, tiled=True),
            lax.all_gather(parent_hess, ("dp", "sub"), axis=0, tiled=True),
        ),
    )
    both_par_grad = par_grad.reshape(slab, nbins, kdim)
    first = split_gains(small_grad, small_hess, sign_vec, low[0], high[0])
    second = split_gains(
        both_par_grad - small_grad, par_hess - small_hess, sign_vec, low[1], high[1]
    )
    gain = jnp.stack([first, second], axis=1)
    return gain[None]


def solution(mesh):
    return jax.shard_map(
        per_device,
        mesh=mesh,
        in_specs=(
            P(("groups", "dp", "sub"), "feat"),
            P(("groups", "dp", "sub"), None),
            P(("groups", "dp", "sub")),
            P(("groups", "dp", "sub")),
            P("groups"),
            P("groups"),
            P("groups"),
            P(("groups", "dp", "sub"), "feat", None),
            P(("groups", "dp", "sub"), "feat", None),
            P("groups"),
            P("groups"),
        ),
        out_specs=P(("groups", "dp", "sub"), "feat", None, None),
        check_vma=False,
    )
```

profile of v0, /device:TPU:0, one launch (start us, length us, event | category | flops | bytes accessed | tf_op | source)
XLA Modules:
  0.0 926.7 jit_solution(11867569497576097602)
XLA Ops:
  23.0 501.4 %while.11 = (s32[]{:T(128)}, f32[32,33,2048]{2,1,0:T(8,128)}, s32[32,2048,16]{1,2,0:T(8,128)}, bf16[33,2048]{1,0:T(8,128)(2,1)S(1)}, s32[]{:T(128)}) while((s32[]{:T(128)}, f32[32,33,2048]{2,1,0:T(8,128)}, s32[32,2048,16]{1,2,0:T(8,128)}, bf16[33,2048]{1,0:T(8,128)(2,1)S(1)}, s32[]{:T(128)}) %tuple.36), condition=%wide.region_2.3_spmd.clone, body=%wide.region_1.2_spmd.clone.sunk | while | flops 281018368 | bytes 34689600 | solution.py:83
  44.6 9.8 %fusion.19 = f32[32,33,2048]{2,1,0:T(8,128)} fusion(f32[32,33,2048]{2,1,0:T(8,128)} %get-tuple-element.105, s32[]{:T(128)} %get-tuple-element.104, bf16[33,2048]{1,0:T(8,128)(2,1)S(1)} %get-tuple-element.112, s32[256,8,16,128]{3,2,1,0:T(8,128)S(1)} %bitcast.73, s32[2048]{0:T(1024)S(1)} %iota_bitcast_fusion.2), kind=kOutput, calls=%fused_computation.7.clone.1 | convolution fusion | flops 281018368 | bytes 17248768 | tf_op jit(solution)/shard_map/while/body/eval_jaxpr/dot_general | solution.py:81
  75.9 9.8 %fusion.19 = f32[32,33,2048]{2,1,0:T(8,128)} fusion(f32[32,33,2048]{2,1,0:T(8,128)} %get-tuple-element.105, s32[]{:T(128)} %get-tuple-element.104, bf16[33,2048]{1,0:T(8,128)(2,1)S(1)} %get-tuple-element.112, s32[256,8,16,128]{3,2,1,0:T(8,128)S(1)} %bitcast.73, s32[2048]{0:T(1024)S(1)} %iota_bitcast_fusion.2), kind=kOutput, calls=%fused_computation.7.clone.1 | convolution fusion | flops 281018368 | bytes 17248768 | tf_op jit(solution)/shard_map/while/body/eval_jaxpr/dot_general | solution.py:81
  122.9 9.8 %fusion.19 = f32[32,33,2048]{2,1,0:T(8,128)} fusion(f32[32,33,2048]{2,1,0:T(8,128)} %get-tuple-element.105, s32[]{:T(128)} %get-tuple-element.104, bf16[33,2048]{1,0:T(8,128)(2,1)S(1)} %get-tuple-element.112, s32[256,8,16,128]{3,2,1,0:T(8,128)S(1)} %bitcast.73, s32[2048]{0:T(1024)S(1)} %iota_bitcast_fusion.2), kind=kOutput, calls=%fused_computation.7.clone.1 | convolution fusion | flops 281018368 | bytes 17248768 | tf_op jit(solution)/shard_map/while/body/eval_jaxpr/dot_general | solution.py:81
  169.9 9.8 %fusion.19 = f32[32,33,2048]{2,1,0:T(8,128)} fusion(f32[32,33,2048]{2,1,0:T(8,128)} %get-tuple-element.105, s32[]{:T(128)} %get-tuple-element.104, bf16[33,2048]{1,0:T(8,128)(2,1)S(1)} %get-tuple-element.112, s32[256,8,16,128]{3,2,1,0:T(8,128)S(1)} %bitcast.73, s32[2048]{0:T(1024)S(1)} %iota_bitcast_fusion.2), kind=kOutput, calls=%fused_computation.7.clone.1 | convolution fusion | flops 281018368 | bytes 17248768 | tf_op jit(solution)/shard_map/while/body/eval_jaxpr/dot_general | solution.py:81
  185.6 9.8 %fusion.19 = f32[32,33,2048]{2,1,0:T(8,128)} fusion(f32[32,33,2048]{2,1,0:T(8,128)} %get-tuple-element.105, s32[]{:T(128)} %get-tuple-element.104, bf16[33,2048]{1,0:T(8,128)(2,1)S(1)} %get-tuple-element.112, s32[256,8,16,128]{3,2,1,0:T(8,128)S(1)} %bitcast.73, s32[2048]{0:T(1024)S(1)} %iota_bitcast_fusion.2), kind=kOutput, calls=%fused_computation.7.clone.1 | convolution fusion | flops 281018368 | bytes 17248768 | tf_op jit(solution)/shard_map/while/body/eval_jaxpr/dot_general | solution.py:81
  201.3 9.8 %fusion.19 = f32[32,33,2048]{2,1,0:T(8,128)} fusion(f32[32,33,2048]{2,1,0:T(8,128)} %get-tuple-element.105, s32[]{:T(128)} %get-tuple-element.104, bf16[33,2048]{1,0:T(8,128)(2,1)S(1)} %get-tuple-element.112, s32[256,8,16,128]{3,2,1,0:T(8,128)S(1)} %bitcast.73, s32[2048]{0:T(1024)S(1)} %iota_bitcast_fusion.2), kind=kOutput, calls=%fused_computation.7.clone.1 | convolution fusion | flops 281018368 | bytes 17248768 | tf_op jit(solution)/shard_map/while/body/eval_jaxpr/dot_general | solution.py:81
  248.2 9.8 %fusion.19 = f32[32,33,2048]{2,1,0:T(8,128)} fusion(f32[32,33,2048]{2,1,0:T(8,128)} %get-tuple-element.105, s32[]{:T(128)} %get-tuple-element.104, bf16[33,2048]{1,0:T(8,128)(2,1)S(1)} %get-tuple-element.112, s32[256,8,16,128]{3,2,1,0:T(8,128)S(1)} %bitcast.73, s32[2048]{0:T(1024)S(1)} %iota_bitcast_fusion.2), kind=kOutput, calls=%fused_computation.7.clone.1 | convolution fusion | flops 281018368 | bytes 17248768 | tf_op jit(solution)/shard_map/while/body/eval_jaxpr/dot_general | solution.py:81
  263.9 9.8 %fusion.19 = f32[32,33,2048]{2,1,0:T(8,128)} fusion(f32[32,33,2048]{2,1,0:T(8,128)} %get-tuple-element.105, s32[]{:T(128)} %get-tuple-element.104, bf16[33,2048]{1,0:T(8,128)(2,1)S(1)} %get-tuple-element.112, s32[256,8,16,128]{3,2,1,0:T(8,128)S(1)} %bitcast.73, s32[2048]{0:T(1024)S(1)} %iota_bitcast_fusion.2), kind=kOutput, calls=%fused_computation.7.clone.1 | convolution fusion | flops 281018368 | bytes 17248768 | tf_op jit(solution)/shard_map/while/body/eval_jaxpr/dot_general | solution.py:81
  279.6 9.8 %fusion.19 = f32[32,33,2048]{2,1,0:T(8,128)} fusion(f32[32,33,2048]{2,1,0:T(8,128)} %get-tuple-element.105, s32[]{:T(128)} %get-tuple-element.104, bf16[33,2048]{1,0:T(8,128)(2,1)S(1)} %get-tuple-element.112, s32[256,8,16,128]{3,2,1,0:T(8,128)S(1)} %bitcast.73, s32[2048]{0:T(1024)S(1)} %iota_bitcast_fusion.2), kind=kOutput, calls=%fused_computation.7.clone.1 | convolution fusion | flops 281018368 | bytes 17248768 | tf_op jit(solution)/shard_map/while/body/eval_jaxpr/dot_general | solution.py:81
  373.6 9.8 %fusion.19 = f32[32,33,2048]{2,1,0:T(8,128)} fusion(f32[32,33,2048]{2,1,0:T(8,128)} %get-tuple-element.105, s32[]{:T(128)} %get-tuple-element.104, bf16[33,2048]{1,0:T(8,128)(2,1)S(1)} %get-tuple-element.112, s32[256,8,16,128]{3,2,1,0:T(8,128)S(1)} %bitcast.73, s32[2048]{0:T(1024)S(1)} %iota_bitcast_fusion.2), kind=kOutput, calls=%fused_computation.7.clone.1 | convolution fusion | flops 281018368 | bytes 17248768 | tf_op jit(solution)/shard_map/while/body/eval_jaxpr/dot_general | solution.py:81
  389.2 9.8 %fusion.19 = f32[32,33,2048]{2,1,0:T(8,128)} fusion(f32[32,33,2048]{2,1,0:T(8,128)} %get-tuple-element.105, s32[]{:T(128)} %get-tuple-element.104, bf16[33,2048]{1,0:T(8,128)(2,1)S(1)} %get-tuple-element.112, s32[256,8,16,128]{3,2,1,0:T(8,128)S(1)} %bitcast.73, s32[2048]{0:T(1024)S(1)} %iota_bitcast_fusion.2), kind=kOutput, calls=%fused_computation.7.clone.1 | convolution fusion | flops 281018368 | bytes 17248768 | tf_op jit(solution)/shard_map/while/body/eval_jaxpr/dot_general | solution.py:81
  404.9 9.8 %fusion.19 = f32[32,33,2048]{2,1,0:T(8,128)} fusion(f32[32,33,2048]{2,1,0:T(8,128)} %get-tuple-element.105, s32[]{:T(128)} %get-tuple-element.104, bf16[33,2048]{1,0:T(8,128)(2,1)S(1)} %get-tuple-element.112, s32[256,8,16,128]{3,2,1,0:T(8,128)S(1)} %bitcast.73, s32[2048]{0:T(1024)S(1)} %iota_bitcast_fusion.2), kind=kOutput, calls=%fused_computation.7.clone.1 | convolution fusion | flops 281018368 | bytes 17248768 | tf_op jit(solution)/shard_map/while/body/eval_jaxpr/dot_general | solution.py:81
  420.6 9.8 %fusion.19 = f32[32,33,2048]{2,1,0:T(8,128)} fusion(f32[32,33,2048]{2,1,0:T(8,128)} %get-tuple-element.105, s32[]{:T(128)} %get-tuple-element.104, bf16[33,2048]{1,0:T(8,128)(2,1)S(1)} %get-tuple-element.112, s32[256,8,16,128]{3,2,1,0:T(8,128)S(1)} %bitcast.73, s32[2048]{0:T(1024)S(1)} %iota_bitcast_fusion.2), kind=kOutput, calls=%fused_computation.7.clone.1 | convolution fusion | flops 281018368 | bytes 17248768 | tf_op jit(solution)/shard_map/while/body/eval_jaxpr/dot_general | solution.py:81
  467.6 9.8 %fusion.19 = f32[32,33,2048]{2,1,0:T(8,128)} fusion(f32[32,33,2048]{2,1,0:T(8,128)} %get-tuple-element.105, s32[]{:T(128)} %get-tuple-element.104, bf16[33,2048]{1,0:T(8,128)(2,1)S(1)} %get-tuple-element.112, s32[256,8,16,128]{3,2,1,0:T(8,128)S(1)} %bitcast.73, s32[2048]{0:T(1024)S(1)} %iota_bitcast_fusion.2), kind=kOutput, calls=%fused_computation.7.clone.1 | convolution fusion | flops 281018368 | bytes 17248768 | tf_op jit(solution)/shard_map/while/body/eval_jaxpr/dot_general | solution.py:81
  498.9 9.8 %fusion.19 = f32[32,33,2048]{2,1,0:T(8,128)} fusion(f32[32,33,2048]{2,1,0:T(8,128)} %get-tuple-element.105, s32[]{:T(128)} %get-tuple-element.104, bf16[33,2048]{1,0:T(8,128)(2,1)S(1)} %get-tuple-element.112, s32[256,8,16,128]{3,2,1,0:T(8,128)S(1)} %bitcast.73, s32[2048]{0:T(1024)S(1)} %iota_bitcast_fusion.2), kind=kOutput, calls=%fused_computation.7.clone.1 | convolution fusion | flops 281018368 | bytes 17248768 | tf_op jit(solution)/shard_map/while/body/eval_jaxpr/dot_general | solution.py:81
  514.6 9.8 %fusion.19 = f32[32,33,2048]{2,1,0:T(8,128)} fusion(f32[32,33,2048]{2,1,0:T(8,128)} %get-tuple-element.105, s32[]{:T(128)} %get-tuple-element.104, bf16[33,2048]{1,0:T(8,128)(2,1)S(1)} %get-tuple-element.112, s32[256,8,16,128]{3,2,1,0:T(8,128)S(1)} %bitcast.73, s32[2048]{0:T(1024)S(1)} %iota_bitcast_fusion.2), kind=kOutput, calls=%fused_computation.7.clone.1 | convolution fusion | flops 281018368 | bytes 17248768 | tf_op jit(solution)/shard_map/while/body/eval_jaxpr/dot_general | solution.py:81
  524.4 9.8 %reshape.265 = f32[32,33,16,128]{3,2,1,0:T(8,128)} reshape(f32[32,33,2048]{2,1,0:T(8,128)} %get-tuple-element.32) | data formatting | bytes 17301504 | tf_op jit(solution)/shard_map/reshape | solution.py:83
  551.7 16.3 %copy.54 = f32[8,64,128,32]{1,3,2,0:T(8,128)} copy(f32[8,64,128,32]{2,1,0,3:T(8,128)} %slice.50) | data formatting | bytes 16777216
  577.1 16.8 %all_gather.7 = f32[8,64,128]{2,1,0:T(8,128)S(1)} all-gather(f32[1,64,128]{2,1,0:T(8,128)S(1)} %copy-done.5), channel_id=1, replica_groups=mesh['groups'=2,'dp'=4,'feat'=2,'sub'=2] {'dp','sub'}, dimensions={0}, use_global_device_ids=true | all-gather | bytes 294912 | tf_op jit(solution)/shard_map/all_gather | solution.py:103
  600.2 58.5 %all-gather.2.cloned.1.call-done = f32[8,64,4096]{2,1,0:T(8,128)} async-done(((f32[1,64,4096]{2,1,0:T(8,128)}), f32[8,64,4096]{2,1,0:T(8,128)}) %all-gather.2.cloned.1.call-update) | async-done | bytes 8388624 | tf_op jit(solution)/shard_map/all_gather | solution.py:102
  665.1 163.1 %reduce-scatter.3.cloned.1.call-done = f32[1,64,4096]{1,2,0:T(8,128)} async-done(((f32[8,64,4096]{1,2,0:T(8,128)}), f32[1,64,4096]{1,2,0:T(8,128)}) %reduce-scatter.3.cloned.1.call-update) | async-done | bytes 1048592 | tf_op jit(solution)/shard_map/reduce_scatter | solution.py:88
  842.9 66.0 %fusion.11 = f32[64,128,32]{2,0,1:T(8,128)S(1)} fusion(f32[64,128,32]{2,0,1:T(8,128)S(1)} %copy-done.2), kind=kOutput, calls=%fused_computation.60 | output fusion | flops 33292288 | bytes 2097152 | tf_op jit(solution)/shard_map/jit(cumsum)/reduce_window_sum | solution.py:16
  909.0 10.4 %multiply_reduce_fusion.1 = (f32[64,128]{0,1:T(8,128)S(1)}, f32[64,128]{0,1:T(8,128)S(1)}, f32[64,128]{0,1:T(8,128)S(1)}, f32[64,128]{0,1:T(8,128)S(1)}) fusion(f32[64,128,32]{2,0,1:T(8,128)S(1)} %fusion.12, f32[64,128]{0,1:T(8,128)S(1)} %copy.50, f32[64]{0:T(128)S(1)} %get-tuple-element.64, f32[64]{0:T(128)S(1)} %get-tuple-element.62, ...), kind=kLoop, calls=%fused_computation.12 | loop fusion | flops 9928704 | bytes 2377728 | tf_op jit(solution)/shard_map/reduce_sum | solution.py:12
  (225 shorter events, 409.6 us)
Async XLA Ops:
  6.5 569.1 %copy-start = (s32[1024]{0:T(1024)S(1)}, s32[1024]{0:T(1024)}, u32[]{:S(2)}) copy-start(s32[1024]{0:T(1024)} %param.17) | copy-start | bytes 12292
  6.5 590.6 %reduce-scatter.5.cloned.1.call-start = ((), (), s32[]{:S(2)}) async-start(), calls=%async_computation.3 | async-start | bytes 294912 | tf_op jit(solution)/shard_map/reduce_scatter | solution.py:89
  7.4 5.6 copy-start.7
  7.4 5.6 copy-start.6
  18.0 5.0 copy-start.4
  538.7 3.3 copy-start.1
  542.7 116.0 %all-gather.2.cloned.1.call-start = ((), (), s32[]{:S(2)}) async-start(), calls=%async_computation.4 | async-start | bytes 9437184 | tf_op jit(solution)/shard_map/all_gather | solution.py:102
  543.5 284.8 %reduce-scatter.3.cloned.1.call-start = ((), (), s32[]{:S(2)}) async-start(), calls=%async_computation.2 | async-start | bytes 18874368 | tf_op jit(solution)/shard_map/reduce_scatter | solution.py:88
  568.0 2.6 copy-start.8
  568.0 3.3 copy-start.9
  568.0 7.1 copy-start.10
  568.0 9.1 copy-start.5
  828.2 3.9 copy-start.3
  839.5 3.4 copy-start.2
Sparse Core Ops, SparseCore 0:
  542.8 33.0 reduce-scatter.4
  577.6 81.0 all-gather.1
  661.2 166.9 reduce-scatter.2
where the time goes:
time: 928 us; the launch traced here: 927 us
  matrix products  314 us (34%)
  local copies, waits for them, and re-layouts  256 us (28%)
  waiting for transfers between devices  222 us (24%)
  other arithmetic  99 us (11%)
  between operations  18.5 us (2%)
  blocking collectives  16.8 us (2%)
    dot_general x32, matrix products, block_sums(): return jnp.dot(weighted, onehot, preferred_element_type=jnp.float32)  314 us
    eq x128, local copies, waits for them, and re-layouts, block_sums(): block[:, :, None] == levels  187 us
    reduce_scatter x1, waiting for transfers between devices, per_device(): lax.psum_scatter(term_grad, ('dp', 'sub'), scatter_dimension=0, tiled=True)  163 us
    another operation x2, other arithmetic, split_gains(): left_grad = jnp.cumsum(grad_hist, axis=1)  68.7 us
    all_gather x1, waiting for transfers between devices, per_device(): lax.all_gather(parent_grad, ('dp', 'sub'), axis=0, tiled=True)  58.5 us
    unnamed x24, local copies, waits for them, and re-layouts  25.7 us
  transfers between devices with their start and end apart: 3, of which 2 were waited for; matrix products, arithmetic and copies ran while one was open for 4% of the time, Pallas kernels for 0%

commit v1 on v0

v1 whole, which is shorter than its diff:
```python
import functools

import jax
import jax.numpy as jnp
from jax import lax
from jax.experimental import pallas as pl
from jax.experimental.pallas import tpu as pltpu
from jax.sharding import PartitionSpec as P

reg_lambda = 1.0
CHUNKS = 2
TILE = 256
MIB = 1024 * 1024
VMEM_SPEC = pl.BlockSpec(memory_space=pltpu.VMEM)
SMEM_SPEC = pl.BlockSpec(memory_space=pltpu.SMEM)


def plan_of(line):
    roles = []
    for z in range(line):
        mine = []
        for step in range(line - 1):
            if z <= step:
                mine.append(("R", step, line - 1 - step + z))
            if line - 1 - z <= step:
                mine.append(("L", step, step - (line - 1 - z)))
        mine.append(("F", line - 1, z))
        roles.append(mine)
    return roles


def prep_kernel(line, slab, place_ref, owner_ref, bins_ref, grads_ref, hess_ref, side_ref, own_ref, send_ref, wt_ref, wt_send_ref, perm_ref):
    f_dev = bins_ref.shape[1]
    half = f_dev // 2
    kdim = grads_ref.shape[1]

    @pl.when(pl.program_id(0) == 0)
    def _():
        z, core = place_ref[0], place_ref[1]
        column = lax.broadcasted_iota(jnp.int32, (1, f_dev), 1)
        position = lax.rem(column, half) // slab
        table = plan_of(line)
        chip = jnp.zeros_like(column)
        for p in range(line):
            target = jnp.int32(0)
            for zz in range(line):
                target = jnp.where(z == zz, jnp.int32(table[zz][p][2]), target)
            chip = jnp.where(position == p, target, chip)
        owner = 2 * chip + jnp.where(column < half, core, 1 - core)
        source = jnp.zeros_like(column)
        for q in range(2 * line):
            source = jnp.where(owner == owner_ref[q], q, source)
        source = source * slab + lax.rem(column, slab)
        rows = lax.broadcasted_iota(jnp.int32, (f_dev, f_dev), 0)
        perm_ref[...] = jnp.where(rows == source, 1.0, 0.0).astype(jnp.bfloat16)

    binned = bins_ref[...].astype(jnp.float32).astype(jnp.bfloat16)
    moved = jnp.dot(binned, perm_ref[...], preferred_element_type=jnp.float32)
    own_ref[...] = moved[:, :half].astype(jnp.bfloat16)
    send_ref[...] = moved[:, half:]
    eye_r = lax.broadcasted_iota(jnp.int32, (kdim, kdim), 0)
    eye_c = lax.broadcasted_iota(jnp.int32, (kdim, kdim), 1)
    eye = jnp.where(eye_r == eye_c, 1.0, 0.0).astype(jnp.bfloat16)
    grads_t = lax.dot_general(eye, grads_ref[...], (((1,), (1,)), ((), ())), preferred_element_type=jnp.float32)
    hess_row = jnp.broadcast_to(hess_ref[...].astype(jnp.float32), (8, hess_ref.shape[1]))
    first = lax.broadcasted_iota(jnp.int32, hess_row.shape, 0) == 0
    stacked = jnp.concatenate([grads_t, jnp.where(first, hess_row, 0.0)], axis=0)
    masked = jnp.where(side_ref[...] == 1, stacked, 0.0)
    wt_send_ref[...] = masked
    wt_ref[...] = jnp.concatenate([masked, jnp.zeros((8, masked.shape[1]), jnp.float32)], axis=0).astype(jnp.bfloat16)


def prep(line, slab, place, owners, bins, grads, hess, side):
    rows, f_dev = bins.shape
    kdim = grads.shape[1]
    block = min(rows, 512)
    half = f_dev // 2
    return pl.pallas_call(
        functools.partial(prep_kernel, line, slab),
        grid=(rows // block,),
        in_specs=[
            SMEM_SPEC,
            SMEM_SPEC,
            pl.BlockSpec((block, f_dev), lambda i: (i, 0)),
            pl.BlockSpec((block, kdim), lambda i: (i, 0)),
            pl.BlockSpec((1, block), lambda i: (0, i)),
            pl.BlockSpec((1, block), lambda i: (0, i)),
        ],
        out_specs=[
            pl.BlockSpec((block, half), lambda i: (i, 0)),
            pl.BlockSpec((block, half), lambda i: (i, 0)),
            pl.BlockSpec((kdim + 16, block), lambda i: (0, i)),
            pl.BlockSpec((kdim + 8, block), lambda i: (0, i)),
        ],
        out_shape=[
            jax.ShapeDtypeStruct((rows, half), jnp.bfloat16),
            jax.ShapeDtypeStruct((rows, half), jnp.float32),
            jax.ShapeDtypeStruct((kdim + 16, rows), jnp.bfloat16),
            jax.ShapeDtypeStruct((kdim + 8, rows), jnp.float32),
        ],
        scratch_shapes=[pltpu.VMEM((f_dev, f_dev), jnp.bfloat16)],
        compiler_params=pltpu.CompilerParams(vmem_limit_bytes=24 * MIB),
        cost_estimate=pl.CostEstimate(flops=2 * rows * f_dev * f_dev, bytes_accessed=8 * rows * f_dev, transcendentals=0),
        name="prep",
    )(place, owners, bins, grads, hess, side)


def hist_kernel(first_column, width, levels, parts, kdim, has_init, *refs):
    refs = list(refs)
    lanes = refs[-3].shape[1]
    pairs = [(refs[2 * i], refs[2 * i + 1]) for i in range(parts)]
    init_ref = refs[2 * parts] if has_init else None
    out_ref, rel_ref, wt_ref = refs[-3:]
    half = pairs[0][0].shape[1]
    rows = pairs[0][0].shape[0]
    src = lax.broadcasted_iota(jnp.int32, (half, lanes), 0)
    dst = lax.broadcasted_iota(jnp.int32, (half, lanes), 1)
    spread = jnp.where(src == first_column + lax.rem(dst, width), 1.0, 0.0).astype(jnp.bfloat16)
    lane = lax.broadcasted_iota(jnp.int32, (1, lanes), 1)
    shift = ((lane // width) * levels).astype(jnp.float32)
    for i, (bins_ref, w_ref) in enumerate(pairs):
        for r in range(0, rows, TILE):
            block = bins_ref[r : r + TILE, :].astype(jnp.bfloat16)
            moved = jnp.dot(block, spread, preferred_element_type=jnp.float32)
            rel_ref[i * rows + r : i * rows + r + TILE, :] = (moved - shift).astype(jnp.bfloat16)
        if w_ref.dtype == jnp.bfloat16:
            wt_ref[:, i * rows : (i + 1) * rows] = w_ref[...]
        else:
            part = jnp.concatenate([w_ref[...], jnp.zeros((8, rows), jnp.float32)], axis=0)
            wt_ref[:, i * rows : (i + 1) * rows] = part.astype(jnp.bfloat16)
    tiles = parts * rows // TILE
    one = jnp.ones((TILE, lanes), jnp.bfloat16)
    zero = jnp.zeros((TILE, lanes), jnp.bfloat16)

    def level(b, carry):
        value = jnp.full((TILE, lanes), b.astype(jnp.float32), jnp.float32).astype(jnp.bfloat16)
        total = jnp.zeros((wt_ref.shape[0], lanes), jnp.float32)
        for t in range(tiles):
            hit = rel_ref[t * TILE : (t + 1) * TILE, :] == value
            onehot = jnp.where(hit, one, zero)
            total = total + jnp.dot(wt_ref[:, t * TILE : (t + 1) * TILE], onehot, preferred_element_type=jnp.float32)
        start = pl.multiple_of(b * kdim, kdim)
        grad = total[:kdim, :]
        hess = total[kdim : kdim + 1, :]
        if has_init:
            grad = grad + init_ref[pl.ds(start, kdim), :]
            hess = hess + init_ref[pl.ds(levels * kdim + b, 1), :]
        out_ref[pl.ds(start, kdim), :] = grad
        out_ref[pl.ds(levels * kdim + b, 1), :] = hess
        return carry

    lax.fori_loop(0, levels, level, 0)


def hist(first_column, width, levels, lanes, kdim, pairs, init=None):
    rows = pairs[0][0].shape[0]
    parts = len(pairs)
    operands = [x for pair in pairs for x in pair]
    if init is not None:
        operands.append(init)
    height = levels * (kdim + 1)
    return pl.pallas_call(
        functools.partial(hist_kernel, first_column, width, levels, parts, kdim, init is not None),
        in_specs=[VMEM_SPEC] * len(operands),
        out_specs=VMEM_SPEC,
        out_shape=jax.ShapeDtypeStruct((height, lanes), jnp.float32),
        scratch_shapes=[
            pltpu.VMEM((parts * rows, lanes), jnp.bfloat16),
            pltpu.VMEM((kdim + 16, parts * rows), jnp.bfloat16),
        ],
        compiler_params=pltpu.CompilerParams(vmem_limit_bytes=24 * MIB),
        cost_estimate=pl.CostEstimate(
            flops=2 * 256 * parts * rows * levels * lanes, bytes_accessed=parts * rows * lanes * 4, transcendentals=0
        ),
        name="hist",
    )(*operands)


def parent_kernel(width, levels, kdim, chunks, parent_ref, *out_refs):
    lanes = out_refs[0].shape[1]
    per_tile = 128 // width
    step = 128 // kdim
    for c in range(chunks):
        for tile in range(lanes // 128):
            for b in range(0, levels, step):
                rows = []
                for jj in range(per_tile):
                    bin_at = (tile * per_tile + jj) * levels + b
                    rows.append(parent_ref[c * width : (c + 1) * width, bin_at * kdim : bin_at * kdim + 128])
                block = jnp.concatenate(rows, axis=0) if per_tile > 1 else rows[0]
                out_refs[c][b * kdim : b * kdim + 128, tile * 128 : (tile + 1) * 128] = block.T


def parent_layout(width, levels, lanes, kdim, chunks, parent):
    shape = jax.ShapeDtypeStruct((levels * kdim, lanes), jnp.float32)
    return pl.pallas_call(
        functools.partial(parent_kernel, width, levels, kdim, chunks),
        in_specs=[VMEM_SPEC],
        out_specs=[VMEM_SPEC] * chunks,
        out_shape=[shape] * chunks,
        compiler_params=pltpu.CompilerParams(vmem_limit_bytes=16 * MIB),
        cost_estimate=pl.CostEstimate(flops=0, bytes_accessed=2 * parent.size * 4, transcendentals=0),
        name="parent_layout",
    )(parent)


def lane_prefix(total, width):
    lanes = total.shape[1]
    lane = lax.broadcasted_iota(jnp.int32, total.shape, 1)
    running = total
    reach = width
    while reach < lanes:
        running = running + jnp.where(lane >= reach, pltpu.roll(running, reach, 1), 0.0)
        reach *= 2
    whole = total
    reach = width
    while reach < lanes:
        whole = whole + pltpu.roll(whole, reach, 1)
        reach *= 2
    return running - total, running, whole


def gain_kernel(width, levels, kdim, last_ref, right_ref, left_ref, par_grad_ref, par_hess_ref, sign_ref, bound_ref, out_ref, grad_ref, hess_ref):
    hess_at = levels * kdim
    lanes = out_ref.shape[2]

    def small_at(start, size):
        return last_ref[pl.ds(start, size), :] + right_ref[pl.ds(start, size), :] + left_ref[pl.ds(start, size), :]

    sign = sign_ref[...]
    small_hess = small_at(hess_at, levels)
    hess_ref[0] = small_hess
    hess_ref[1] = par_hess_ref[...] - small_hess

    def add_up(b, carry):
        g0, g1, h0, h1 = carry
        start = pl.multiple_of(b * kdim, kdim)
        small = small_at(start, kdim)
        g0 = g0 + small
        g1 = g1 + (par_grad_ref[pl.ds(start, kdim), :] - small)
        h0 = h0 + hess_ref[0, pl.ds(b, 1), :]
        h1 = h1 + hess_ref[1, pl.ds(b, 1), :]
        grad_ref[0, pl.ds(start, kdim), :] = g0
        grad_ref[1, pl.ds(start, kdim), :] = g1
        hess_ref[0, pl.ds(b, 1), :] = h0
        hess_ref[1, pl.ds(b, 1), :] = h1
        return g0, g1, h0, h1

    zero_g = jnp.zeros((kdim, lanes), jnp.float32)
    zero_h = jnp.zeros((1, lanes), jnp.float32)
    ends = lax.fori_loop(0, levels, add_up, (zero_g, zero_g, zero_h, zero_h))
    for c in range(2):
        low = bound_ref[0, c].astype(jnp.float32) / 1024.0
        high = bound_ref[1, c].astype(jnp.float32) / 1024.0
        middle = 0.5 * (low + high)
        low_left = jnp.where(sign < 0, middle, low)
        high_left = jnp.where(sign > 0, middle, high)
        low_right = jnp.where(sign > 0, middle, low)
        high_right = jnp.where(sign < 0, middle, high)
        grad_before, _, grad_all = lane_prefix(ends[c], width)
        hess_rows = jnp.broadcast_to(ends[2 + c], (8, lanes))
        hess_before, _, hess_all = lane_prefix(hess_rows, width)
        hess_before, hess_all = hess_before[:1], hess_all[:1]

        def score(grad, hess, lower, upper):
            denom = jnp.maximum(hess, 0.0) + reg_lambda
            weight = jnp.clip(-grad / denom, lower, upper)
            return jnp.sum((2.0 * grad + denom * weight) * weight, axis=0, keepdims=True)

        def one_bin(b, carry):
            start = pl.multiple_of(b * kdim, kdim)
            grad_left = grad_ref[c, pl.ds(start, kdim), :] + grad_before
            hess_left = hess_ref[c, pl.ds(b, 1), :] + hess_before
            left = score(grad_left, hess_left, low_left, high_left)
            right = score(grad_all - grad_left, hess_all - hess_left, low_right, high_right)
            out_ref[c, pl.ds(b, 1), :] = (left + right) * (-1.0 / kdim)
            return carry

        lax.fori_loop(0, levels, one_bin, 0)


def gains_of(width, levels, lanes, kdim, last, right, left, par_grad, par_hess, sign, bounds):
    return pl.pallas_call(
        functools.partial(gain_kernel, width, levels, kdim),
        in_specs=[VMEM_SPEC] * 6 + [SMEM_SPEC],
        out_specs=VMEM_SPEC,
        out_shape=jax.ShapeDtypeStruct((2, levels, lanes), jnp.float32),
        scratch_shapes=[
            pltpu.VMEM((2, levels * kdim, lanes), jnp.float32),
            pltpu.VMEM((2, levels, lanes), jnp.float32),
        ],
        compiler_params=pltpu.CompilerParams(vmem_limit_bytes=24 * MIB),
        cost_estimate=pl.CostEstimate(flops=50 * levels * kdim * lanes, bytes_accessed=16 * levels * kdim * lanes, transcendentals=0),
        name="gains",
    )(last, right, left, par_grad, par_hess, sign, bounds)


def inverse_of(owner, slots):
    return jnp.sum(jnp.where(owner[None, :] == slots[:, None], slots[None, :], 0), axis=1)


def one_of(z, members):
    hit = z == members[0]
    for m in members[1:]:
        hit = hit | (z == m)
    return hit


def per_device(bins, grads, hess, node_side, signs, child_owner, parent_owner, parent_grad, parent_hess, node_low, node_high):
    line = lax.axis_size("dp")
    owners = line * lax.axis_size("sub")
    z = lax.axis_index("dp")
    core = lax.axis_index("sub")
    place = lax.axis_index(("dp", "sub"))
    column = lax.axis_index("feat")
    rows, f_dev = bins.shape
    kdim = grads.shape[1]
    nbins = parent_hess.shape[2]
    slab = parent_grad.shape[1]
    chunks = CHUNKS if slab >= 32 else 1
    width = slab // chunks
    lanes = min(256, width * nbins * kdim // 128)
    groups = lanes // width
    levels = nbins // groups
    plan = plan_of(line)

    where = jnp.stack([z, core]).astype(jnp.int32)
    own, send, wt, wt_send = prep(
        line, slab, where, parent_owner, bins, grads, hess.reshape(1, rows), node_side.reshape(1, rows)
    )
    swap = [(0, 1), (1, 0)]
    other = lax.ppermute(send, "sub", swap)
    wt_other = lax.ppermute(wt_send, "sub", swap)

    units = {}
    for c in range(chunks):
        units[0, c] = hist(c * width, width, levels, lanes, kdim, [(own, wt)])
    for c in range(chunks):
        units[0, c] = hist(c * width, width, levels, lanes, kdim, [(other, wt_other)], units[0, c])

    def pick(kind, step, c):
        where_at = {}
        for zz in range(line):
            for p, role in enumerate(plan[zz]):
                if role[:2] == (kind, step):
                    where_at.setdefault(p, []).append(zz)
        spots = sorted(where_at)
        value = units[spots[0], c]
        for p in spots[1:]:
            value = jnp.where(one_of(z, where_at[p]), units[p, c], value)
        return value

    slots = jnp.arange(owners, dtype=jnp.int32)
    parent_inv = inverse_of(parent_owner, slots)
    my_slab = parent_inv[place]
    ids = column * f_dev + my_slab * slab
    my_signs = lax.dynamic_slice(signs, (ids,), (slab,)).reshape(chunks, 1, width)
    my_signs = jnp.tile(my_signs, (1, 1, groups))
    bounds = jnp.stack([node_low, node_high])
    par_hess = jnp.transpose(parent_hess[0].reshape(chunks, width, groups, levels), (0, 3, 2, 1)).reshape(chunks, levels, lanes)
    par_grad = parent_layout(width, levels, lanes, kdim, chunks, parent_grad[0])

    from_left = [None] * chunks
    from_right = [None] * chunks
    for step in range(line - 1):
        if step > 0:
            for c in range(chunks):
                units[step, c] = hist(step * slab + c * width, width, levels, lanes, kdim, [(own, wt), (other, wt_other)])
        for c in range(chunks):
            to_right = pick("R", step, c)
            to_left = pick("L", step, c)
            if step > 0:
                to_right = to_right + from_left[c]
                to_left = to_left + from_right[c]
            from_left[c] = lax.ppermute(to_right, "dp", [(i, i + 1) for i in range(step + 1)])
            from_right[c] = lax.ppermute(to_left, "dp", [(line - 1 - i, line - 2 - i) for i in range(step + 1)])
    last = line - 1
    for c in range(chunks):
        units[last, c] = hist(last * slab + c * width, width, levels, lanes, kdim, [(own, wt), (other, wt_other)])

    child_inv = inverse_of(child_owner, slots)
    source_of = jnp.sum(jnp.where(child_inv[:, None] == slots[None, :], parent_owner[None, :], 0), axis=1)
    pair = 2 * z
    my_source = source_of[place]
    twin_source = source_of[pair + 1 - core]
    done = []
    for c in range(chunks):
        gain = gains_of(width, levels, lanes, kdim, units[last, c], from_left[c], from_right[c], par_grad[c], par_hess[c], my_signs[c], bounds)
        got = [gain] + [lax.ppermute(gain, "dp", [(i, (i + s) % line) for i in range(line)]) for s in range(1, line)]

        def choose(source):
            chip = source // 2
            value = got[0]
            for s in range(1, line):
                value = jnp.where(lax.rem(z - chip + line, line) == s, got[s], value)
            return value

        crossed = lax.ppermute(choose(twin_source), "sub", swap)
        gain = jnp.where(lax.rem(my_source, 2) == core, choose(my_source), crossed)
        gain = jnp.transpose(gain.reshape(2, levels, groups, width), (3, 0, 2, 1))
        done.append(gain.reshape(width, 2, nbins))
    return jnp.concatenate(done, axis=0)[None]


def solution(mesh):
    return jax.shard_map(
        per_device,
        mesh=mesh,
        in_specs=(
            P(("groups", "dp", "sub"), "feat"),
            P(("groups", "dp", "sub"), None),
            P(("groups", "dp", "sub")),
            P(("groups", "dp", "sub")),
            P("groups"),
            P("groups"),
            P("groups"),
            P(("groups", "dp", "sub"), "feat", None),
            P(("groups", "dp", "sub"), "feat", None),
            P("groups"),
            P("groups"),
        ),
        out_specs=P(("groups", "dp", "sub"), "feat", None, None),
        check_vma=False,
    )
```

time: 928 us -> 159 us (0.17)
  matrix products: 314 us -> 0 us
  local copies, waits for them, and re-layouts: 256 us -> 10.7 us
  waiting for transfers between devices: 222 us -> 6.27 us
  other arithmetic: 99 us -> 1.1 us
  Pallas kernels: 0 us -> 93.7 us
  starting transfers between devices: 0.08 us -> 40.2 us
  blocking collectives: 16.8 us -> 0 us
  between operations: 18.5 us -> 6.14 us
    dot_general x32 -> x0, matrix products: 314 us -> none  [block_sums(): return jnp.dot(weighted, onehot, preferred_element_type=jnp.float32)]
    eq x128 -> x0, local copies, waits for them, and re-layouts: 187 us -> none  [block_sums(): block[:, :, None] == levels]
    reduce_scatter x2 -> x0, waiting for transfers between devices: 163 us -> none  [the longest x1 163 us: per_device(): lax.psum_scatter(term_grad, ('dp', 'sub'), scatter_dimension=0, tiled=True)]
    pallas_call x0 -> x14, Pallas kernels: none -> 93.7 us  [the longest x10 84.3 us: hist(): pl.pallas_call(functools.partial(hist_kernel, first_column, width, levels...]
    another operation x4 -> x2, other arithmetic: 70 us -> 0.08 us  [the longest x1 0.07 us: per_device(): where = jnp.stack([z, core]).astype(jnp.int32)]
    all_gather x1 -> x0, waiting for transfers between devices: 58.5 us -> none  [per_device(): lax.all_gather(parent_grad, ('dp', 'sub'), axis=0, tiled=True)]
    ppermute x0 -> x22, starting transfers between devices: none -> 40.2 us  [the longest x6 22 us: per_device(): lax.ppermute(to_right, 'dp', [(i, i + 1) for i in range(step + 1)])]
    unnamed x24, local copies, waits for them, and re-layouts: 25.7 us -> 6.43 us
  transfers between devices with their start and end apart: 3 -> 22, of which waited for: 2 -> 5; matrix products, arithmetic and copies ran while one was open for 4% -> 2% of each run, Pallas kernels for 0% -> 53%
where the time goes in v1:
time: 159 us; the launch traced here: 158 us
  Pallas kernels  93.7 us (59%)
  starting transfers between devices  40.2 us (25%)
  local copies, waits for them, and re-layouts  10.7 us (7%)
  waiting for transfers between devices  6.27 us (4%)
  between operations  6.14 us (4%)
    pallas_call x10, Pallas kernels, hist(): pl.pallas_call(functools.partial(hist_kernel, first_column, width, levels...  84.3 us
    ppermute x6, starting transfers between devices, per_device(): lax.ppermute(to_right, 'dp', [(i, i + 1) for i in range(step + 1)])  22 us
    ppermute x6, starting transfers between devices, per_device(): lax.ppermute(gain, 'dp', [(i, (i + s) % line) for i in range(line)])  12.2 us
    unnamed x24, local copies, waits for them, and re-layouts  6.43 us
    ppermute x6, starting transfers between devices, per_device(): lax.ppermute(to_left, 'dp', [(line - 1 - i, line - 2 - i) for i in range(...  5.37 us
    pallas_call x2, Pallas kernels, gains_of(): pl.pallas_call(functools.partial(gain_kernel, width, levels, kdim), in_sp...  5.34 us
    ppermute x6, waiting for transfers between devices, per_device(): lax.ppermute(gain, 'dp', [(i, (i + s) % line) for i in range(line)])  4.98 us
    pallas_call x1, Pallas kernels, prep(): pl.pallas_call(functools.partial(prep_kernel, line, slab), grid=(rows //...  3.77 us
  transfers between devices with their start and end apart: 22, of which 5 were waited for; matrix products, arithmetic and copies ran while one was open for 2% of the time, Pallas kernels for 53%

profile of v1, /device:TPU:0, one launch (start us, length us, event | category | flops | bytes accessed | tf_op | source)
XLA Modules:
  0.0 158.1 jit_solution(14917460560689311470)
XLA Ops:
  2.0 2.2 %copy-done = s32[2048,512]{1,0:T(8,128)S(1)} copy-done((s32[2048,512]{1,0:T(8,128)S(1)}, s32[2048,512]{1,0:T(8,128)}, u32[]{:S(2)}) %copy-start) | copy-done | bytes 4194328
  5.5 3.8 %prep.1 = (bf16[2048,256]{1,0:T(8,128)(2,1)S(1)}, f32[2048,256]{1,0:T(8,128)}, bf16[48,2048]{1,0:T(8,128)(2,1)S(1)}, f32[40,2048]{1,0:T(8,128)}) custom-call(s32[2]{0:T(128)S(1)} %pad_add_fusion.1.place_ref, s32[8]{0:T(128)S(1)} %copy-done.3, s32[2048,512]{1,0:T(8,128)S(1)} %copy-done, bf16[2048,32]{1,0:T(8,128)(2,1)S(1)} %copy.23.grads_ref, ...), custom_call_target="tpu_custom_call" | custom-call | flops 1073741824 | bytes 8388608 | tf_op jit(solution)/shard_map/prep/pallas_call | solution.py:78
  20.5 5.2 %hist.13.refs_2_ = f32[528,256]{1,0:T(8,128)S(1)} custom-call(bf16[2048,256]{1,0:T(8,128)(2,1)S(1)} %get-tuple-element.11.refs_0_, bf16[48,2048]{1,0:T(8,128)(2,1)S(1)} %copy-done.6), custom_call_target="tpu_custom_call" | custom-call | flops 4294967296 | bytes 2097152 | tf_op jit(solution)/shard_map/hist/pallas_call | solution.py:162
  25.7 5.2 %hist.18.refs_2_ = f32[528,256]{1,0:T(8,128)S(1)} custom-call(bf16[2048,256]{1,0:T(8,128)(2,1)S(1)} %get-tuple-element.11.refs_0_, bf16[48,2048]{1,0:T(8,128)(2,1)S(1)} %copy-done.6), custom_call_target="tpu_custom_call" | custom-call | flops 4294967296 | bytes 2097152 | tf_op jit(solution)/shard_map/hist/pallas_call | solution.py:162
  31.0 6.8 %hist.14 = f32[528,256]{1,0:T(8,128)S(1)} custom-call(f32[2048,256]{1,0:T(8,128)} %collective-permute-done.refs_2_.refs_0_, f32[40,2048]{1,0:T(8,128)S(1)} %collective-permute-done.1.refs_3_.refs_1_, f32[528,256]{1,0:T(8,128)S(1)} %hist.13.refs_2_), custom_call_target="tpu_custom_call" | custom-call | flops 4294967296 | bytes 2097152 | tf_op jit(solution)/shard_map/hist/pallas_call | solution.py:162
  37.8 5.0 %collective-permute-start.2 = (f32[528,256]{1,0:T(8,128)S(1)}, f32[528,256]{1,0:T(8,128)S(1)}, u32[]{:S(2)}, u32[]{:S(2)}) collective-permute-start(f32[528,256]{1,0:T(8,128)S(1)} %hist.14), channel_id=1, source_target_pairs={{0,4},{1,5},{2,6},{3,7},{16,20},{17,21},{18,22},{19,23}} | collective-permute-start | bytes 1622024 | tf_op jit(solution)/shard_map/ppermute | solution.py:375
  43.5 6.8 %hist.19 = f32[528,256]{1,0:T(8,128)S(1)} custom-call(f32[2048,256]{1,0:T(8,128)} %collective-permute-done.refs_2_.refs_0_, f32[40,2048]{1,0:T(8,128)S(1)} %collective-permute-done.1.refs_3_.refs_1_, f32[528,256]{1,0:T(8,128)S(1)} %hist.18.refs_2_), custom_call_target="tpu_custom_call" | custom-call | flops 4294967296 | bytes 2097152 | tf_op jit(solution)/shard_map/hist/pallas_call | solution.py:162
  50.4 1.3 collective-permute-start.12
  52.4 10.0 %hist.12 = f32[528,256]{1,0:T(8,128)S(1)} custom-call(bf16[2048,256]{1,0:T(8,128)(2,1)S(1)} %get-tuple-element.11.refs_0_, bf16[48,2048]{1,0:T(8,128)(2,1)S(1)} %copy-done.6, f32[2048,256]{1,0:T(8,128)} %collective-permute-done.refs_2_.refs_0_, f32[40,2048]{1,0:T(8,128)S(1)} %collective-permute-done.1.refs_3_.refs_1_), custom_call_target="tpu_custom_call" | custom-call | flops 8589934592 | bytes 4194304 | tf_op jit(solution)/shard_map/hist/pallas_call | solution.py:162
  62.4 10.0 %hist.11 = f32[528,256]{1,0:T(8,128)S(1)} custom-call(bf16[2048,256]{1,0:T(8,128)(2,1)S(1)} %get-tuple-element.11.refs_0_, bf16[48,2048]{1,0:T(8,128)(2,1)S(1)} %copy-done.6, f32[2048,256]{1,0:T(8,128)} %collective-permute-done.refs_2_.refs_0_, f32[40,2048]{1,0:T(8,128)S(1)} %collective-permute-done.1.refs_3_.refs_1_), custom_call_target="tpu_custom_call" | custom-call | flops 8589934592 | bytes 4194304 | tf_op jit(solution)/shard_map/hist/pallas_call | solution.py:162
  72.5 10.0 %hist.10.last_ref = f32[528,256]{1,0:T(8,128)S(1)} custom-call(bf16[2048,256]{1,0:T(8,128)(2,1)S(1)} %get-tuple-element.11.refs_0_, bf16[48,2048]{1,0:T(8,128)(2,1)S(1)} %copy-done.6, f32[2048,256]{1,0:T(8,128)} %collective-permute-done.refs_2_.refs_0_, f32[40,2048]{1,0:T(8,128)S(1)} %collective-permute-done.1.refs_3_.refs_1_), custom_call_target="tpu_custom_call" | custom-call | flops 8589934592 | bytes 4194304 | tf_op jit(solution)/shard_map/hist/pallas_call | solution.py:162
  82.7 1.3 collective-permute-start.3
  84.7 10.0 %hist.17 = f32[528,256]{1,0:T(8,128)S(1)} custom-call(bf16[2048,256]{1,0:T(8,128)(2,1)S(1)} %get-tuple-element.11.refs_0_, bf16[48,2048]{1,0:T(8,128)(2,1)S(1)} %copy-done.6, f32[2048,256]{1,0:T(8,128)} %collective-permute-done.refs_2_.refs_0_, f32[40,2048]{1,0:T(8,128)S(1)} %collective-permute-done.1.refs_3_.refs_1_), custom_call_target="tpu_custom_call" | custom-call | flops 8589934592 | bytes 4194304 | tf_op jit(solution)/shard_map/hist/pallas_call | solution.py:162
  94.9 4.0 %collective-permute-start.13 = (f32[528,256]{1,0:T(8,128)S(1)}, f32[528,256]{1,0:T(8,128)S(1)}, u32[]{:S(2)}, u32[]{:S(2)}) collective-permute-start(f32[528,256]{1,0:T(8,128)S(1)} %get-tuple-element.22), channel_id=1, source_target_pairs={{0,4},{4,8},{1,5},{5,9},{2,6},{6,10},{3,7},{7,11},{16,20},{20,24},... | collective-permute-start | bytes 1622024 | tf_op jit(solution)/shard_map/ppermute | solution.py:375
  99.8 5.1 %collective-permute-start.4 = (f32[528,256]{1,0:T(8,128)S(1)}, f32[528,256]{1,0:T(8,128)S(1)}, u32[]{:S(2)}, u32[]{:S(2)}) collective-permute-start(f32[528,256]{1,0:T(8,128)S(1)} %get-tuple-element.24), channel_id=1, source_target_pairs={{0,4},{4,8},{8,12},{1,5},{5,9},{9,13},{2,6},{6,10},{10,14},{3,7},{... | collective-permute-start | bytes 1622024 | tf_op jit(solution)/shard_map/ppermute | solution.py:375
  106.2 10.0 %hist.16 = f32[528,256]{1,0:T(8,128)S(1)} custom-call(bf16[2048,256]{1,0:T(8,128)(2,1)S(1)} %get-tuple-element.11.refs_0_, bf16[48,2048]{1,0:T(8,128)(2,1)S(1)} %copy-done.6, f32[2048,256]{1,0:T(8,128)} %collective-permute-done.refs_2_.refs_0_, f32[40,2048]{1,0:T(8,128)S(1)} %collective-permute-done.1.refs_3_.refs_1_), custom_call_target="tpu_custom_call" | custom-call | flops 8589934592 | bytes 4194304 | tf_op jit(solution)/shard_map/hist/pallas_call | solution.py:162
  116.4 5.2 %collective-permute-start.14 = (f32[528,256]{1,0:T(8,128)S(1)}, f32[528,256]{1,0:T(8,128)S(1)}, u32[]{:S(2)}, u32[]{:S(2)}) collective-permute-start(f32[528,256]{1,0:T(8,128)S(1)} %get-tuple-element.26), channel_id=1, source_target_pairs={{0,4},{4,8},{8,12},{1,5},{5,9},{9,13},{2,6},{6,10},{10,14},{3,7},{... | collective-permute-start | bytes 1622024 | tf_op jit(solution)/shard_map/ppermute | solution.py:375
  123.2 2.7 %gains.2 = f32[2,16,256]{2,1,0:T(8,128)S(1)} custom-call(f32[528,256]{1,0:T(8,128)S(1)} %hist.10.last_ref, f32[528,256]{1,0:T(8,128)S(1)} %collective-permute-done.4.right_ref, f32[528,256]{1,0:T(8,128)S(1)} %collective-permute-done.7.left_ref, f32[512,256]{1,0:T(8,128)S(1)} %get-tuple-element.15.par_grad_ref, f32[16,256]{1,0:T(8,128)S(1)} %squeeze.20.par_hess_ref, ...), custom_call_target="tpu_custom_call" | custom-call | flops 6553600 | bytes 2097152 | tf_op jit(solution)/shard_map/gains/pallas_call | solution.py:283
  125.8 7.1 %collective-permute-start.10 = (f32[2,16,256]{2,1,0:T(8,128)S(1)}, f32[2,16,256]{2,1,0:T(8,128)S(1)}, u32[]{:S(2)}, u32[]{:S(2)}) collective-permute-start(f32[2,16,256]{2,1,0:T(8,128)S(1)} %gains.2), channel_id=1, source_target_pairs={{0,4},{4,8},{8,12},{12,0},{1,5},{5,9},{9,13},{13,1},{2,6},{6,10},{... | collective-permute-start | bytes 98312 | tf_op jit(solution)/shard_map/ppermute | solution.py:389
  133.0 1.5 collective-permute-start.9
  134.5 10.0 %hist.15.last_ref = f32[528,256]{1,0:T(8,128)S(1)} custom-call(bf16[2048,256]{1,0:T(8,128)(2,1)S(1)} %get-tuple-element.11.refs_0_, bf16[48,2048]{1,0:T(8,128)(2,1)S(1)} %copy-done.6, f32[2048,256]{1,0:T(8,128)} %collective-permute-done.refs_2_.refs_0_, f32[40,2048]{1,0:T(8,128)S(1)} %collective-permute-done.1.refs_3_.refs_1_), custom_call_target="tpu_custom_call" | custom-call | flops 8589934592 | bytes 4194304 | tf_op jit(solution)/shard_map/hist/pallas_call | solution.py:162
  144.5 2.7 %gains.3 = f32[2,16,256]{2,1,0:T(8,128)S(1)} custom-call(f32[528,256]{1,0:T(8,128)S(1)} %hist.15.last_ref, f32[528,256]{1,0:T(8,128)S(1)} %collective-permute-done.14.right_ref, f32[528,256]{1,0:T(8,128)S(1)} %collective-permute-done.17.left_ref, f32[512,256]{1,0:T(8,128)S(1)} %get-tuple-element.16.par_grad_ref, f32[16,256]{1,0:T(8,128)S(1)} %squeeze.22.par_hess_ref, ...), custom_call_target="tpu_custom_call" | custom-call | flops 6553600 | bytes 2097152 | tf_op jit(solution)/shard_map/gains/pallas_call | solution.py:283
  147.2 2.9 %collective-permute-start.18 = (f32[2,16,256]{2,1,0:T(8,128)S(1)}, f32[2,16,256]{2,1,0:T(8,128)S(1)}, u32[]{:S(2)}, u32[]{:S(2)}) collective-permute-start(f32[2,16,256]{2,1,0:T(8,128)S(1)} %gains.3), channel_id=1, source_target_pairs={{0,12},{4,0},{8,4},{12,8},{1,13},{5,1},{9,5},{13,9},{2,14},{6,2},{... | collective-permute-start | bytes 98312 | tf_op jit(solution)/shard_map/ppermute | solution.py:389
  151.7 3.2 %collective-permute-done.19 = f32[2,16,256]{2,1,0:T(8,128)S(1)} collective-permute-done((f32[2,16,256]{2,1,0:T(8,128)S(1)}, f32[2,16,256]{2,1,0:T(8,128)S(1)}, u32[]{:S(2)}, u32[]{:S(2)}) %collective-permute-start.19) | collective-permute-done | bytes 32800 | tf_op jit(solution)/shard_map/ppermute | solution.py:389
  (91 shorter events, 19.7 us)
Async XLA Ops:
  5.5 13.0 %copy-start.1 = (f32[1,64,4096]{2,1,0:T(8,128)S(1)}, f32[1,64,4096]{2,1,0:T(8,128)}, u32[]{:S(2)}) copy-start(f32[1,64,4096]{2,1,0:T(8,128)} %param.18) | copy-start | bytes 3145732
  5.5 13.4 %copy-start.7 = (f32[1,64,128]{2,1,0:T(8,128)S(1)}, f32[1,64,128]{2,1,0:T(8,128)}, u32[]{:S(2)}) copy-start(f32[1,64,128]{2,1,0:T(8,128)} %param.19) | copy-start | bytes 98308
  10.0 21.0 %collective-permute-start = (f32[2048,256]{1,0:T(8,128)}, f32[2048,256]{1,0:T(8,128)}, u32[]{:S(2)}, u32[]{:S(2)}) collective-permute-start(f32[2048,256]{1,0:T(8,128)} %get-tuple-element.13), channel_id=1, source_target_pairs={{0,1},{1,0},{2,3},{3,2},{4,5},{5,4},{6,7},{7,6},{8,9},{9,8},{10,11... | collective-permute-start | bytes 6291464 | tf_op jit(solution)/shard_map/ppermute | solution.py:332
  10.4 20.6 %collective-permute-start.1 = (f32[40,2048]{1,0:T(8,128)}, f32[40,2048]{1,0:T(8,128)S(1)}, u32[]{:S(2)}, u32[]{:S(2)}) collective-permute-start(f32[40,2048]{1,0:T(8,128)} %get-tuple-element.14), channel_id=1, source_target_pairs={{0,1},{1,0},{2,3},{3,2},{4,5},{5,4},{6,7},{7,6},{8,9},{9,8},{10,11... | collective-permute-start | bytes 983048 | tf_op jit(solution)/shard_map/ppermute | solution.py:333
  37.8 44.7 %collective-permute-start.2 = (f32[528,256]{1,0:T(8,128)S(1)}, f32[528,256]{1,0:T(8,128)S(1)}, u32[]{:S(2)}, u32[]{:S(2)}) collective-permute-start(f32[528,256]{1,0:T(8,128)S(1)} %hist.14), channel_id=1, source_target_pairs={{0,4},{1,5},{2,6},{3,7},{16,20},{17,21},{18,22},{19,23}} | collective-permute-start | bytes 1622024 | tf_op jit(solution)/shard_map/ppermute | solution.py:375
  42.8 39.7 %collective-permute-start.5 = (f32[528,256]{1,0:T(8,128)S(1)}, f32[528,256]{1,0:T(8,128)S(1)}, u32[]{:S(2)}, u32[]{:S(2)}) collective-permute-start(f32[528,256]{1,0:T(8,128)S(1)} %hist.14), channel_id=1, source_target_pairs={{12,8},{13,9},{14,10},{15,11},{28,24},{29,25},{30,26},{31,27}} | collective-permute-start | bytes 1622024 | tf_op jit(solution)/shard_map/ppermute | solution.py:376
  50.4 44.4 %collective-permute-start.12 = (f32[528,256]{1,0:T(8,128)S(1)}, f32[528,256]{1,0:T(8,128)S(1)}, u32[]{:S(2)}, u32[]{:S(2)}) collective-permute-start(f32[528,256]{1,0:T(8,128)S(1)} %hist.19), channel_id=1, source_target_pairs={{0,4},{1,5},{2,6},{3,7},{16,20},{17,21},{18,22},{19,23}} | collective-permute-start | bytes 1622024 | tf_op jit(solution)/shard_map/ppermute | solution.py:375
  51.7 43.0 %collective-permute-start.15 = (f32[528,256]{1,0:T(8,128)S(1)}, f32[528,256]{1,0:T(8,128)S(1)}, u32[]{:S(2)}, u32[]{:S(2)}) collective-permute-start(f32[528,256]{1,0:T(8,128)S(1)} %hist.19), channel_id=1, source_target_pairs={{12,8},{13,9},{14,10},{15,11},{28,24},{29,25},{30,26},{31,27}} | collective-permute-start | bytes 1622024 | tf_op jit(solution)/shard_map/ppermute | solution.py:376
  82.7 17.0 %collective-permute-start.3 = (f32[528,256]{1,0:T(8,128)S(1)}, f32[528,256]{1,0:T(8,128)S(1)}, u32[]{:S(2)}, u32[]{:S(2)}) collective-permute-start(f32[528,256]{1,0:T(8,128)S(1)} %get-tuple-element.20), channel_id=1, source_target_pairs={{0,4},{4,8},{1,5},{5,9},{2,6},{6,10},{3,7},{7,11},{16,20},{20,24},... | collective-permute-start | bytes 1622024 | tf_op jit(solution)/shard_map/ppermute | solution.py:375
  84.0 15.6 %collective-permute-start.6 = (f32[528,256]{1,0:T(8,128)S(1)}, f32[528,256]{1,0:T(8,128)S(1)}, u32[]{:S(2)}, u32[]{:S(2)}) collective-permute-start(f32[528,256]{1,0:T(8,128)S(1)} %get-tuple-element.19), channel_id=1, source_target_pairs={{12,8},{8,4},{13,9},{9,5},{14,10},{10,6},{15,11},{11,7},{28,24},{2... | collective-permute-start | bytes 1622024 | tf_op jit(solution)/shard_map/ppermute | solution.py:376
  94.9 21.4 %collective-permute-start.13 = (f32[528,256]{1,0:T(8,128)S(1)}, f32[528,256]{1,0:T(8,128)S(1)}, u32[]{:S(2)}, u32[]{:S(2)}) collective-permute-start(f32[528,256]{1,0:T(8,128)S(1)} %get-tuple-element.22), channel_id=1, source_target_pairs={{0,4},{4,8},{1,5},{5,9},{2,6},{6,10},{3,7},{7,11},{16,20},{20,24},... | collective-permute-start | bytes 1622024 | tf_op jit(solution)/shard_map/ppermute | solution.py:375
  98.9 17.4 %collective-permute-start.16 = (f32[528,256]{1,0:T(8,128)S(1)}, f32[528,256]{1,0:T(8,128)S(1)}, u32[]{:S(2)}, u32[]{:S(2)}) collective-permute-start(f32[528,256]{1,0:T(8,128)S(1)} %get-tuple-element.21), channel_id=1, source_target_pairs={{12,8},{8,4},{13,9},{9,5},{14,10},{10,6},{15,11},{11,7},{28,24},{2... | collective-permute-start | bytes 1622024 | tf_op jit(solution)/shard_map/ppermute | solution.py:376
  99.8 23.4 %collective-permute-start.4 = (f32[528,256]{1,0:T(8,128)S(1)}, f32[528,256]{1,0:T(8,128)S(1)}, u32[]{:S(2)}, u32[]{:S(2)}) collective-permute-start(f32[528,256]{1,0:T(8,128)S(1)} %get-tuple-element.24), channel_id=1, source_target_pairs={{0,4},{4,8},{8,12},{1,5},{5,9},{9,13},{2,6},{6,10},{10,14},{3,7},{... | collective-permute-start | bytes 1622024 | tf_op jit(solution)/shard_map/ppermute | solution.py:375
  104.9 18.2 %collective-permute-start.7 = (f32[528,256]{1,0:T(8,128)S(1)}, f32[528,256]{1,0:T(8,128)S(1)}, u32[]{:S(2)}, u32[]{:S(2)}) collective-permute-start(f32[528,256]{1,0:T(8,128)S(1)} %get-tuple-element.23), channel_id=1, source_target_pairs={{12,8},{8,4},{4,0},{13,9},{9,5},{5,1},{14,10},{10,6},{6,2},{15,11}... | collective-permute-start | bytes 1622024 | tf_op jit(solution)/shard_map/ppermute | solution.py:376
  116.4 28.1 %collective-permute-start.14 = (f32[528,256]{1,0:T(8,128)S(1)}, f32[528,256]{1,0:T(8,128)S(1)}, u32[]{:S(2)}, u32[]{:S(2)}) collective-permute-start(f32[528,256]{1,0:T(8,128)S(1)} %get-tuple-element.26), channel_id=1, source_target_pairs={{0,4},{4,8},{8,12},{1,5},{5,9},{9,13},{2,6},{6,10},{10,14},{3,7},{... | collective-permute-start | bytes 1622024 | tf_op jit(solution)/shard_map/ppermute | solution.py:375
  121.6 22.9 %collective-permute-start.17 = (f32[528,256]{1,0:T(8,128)S(1)}, f32[528,256]{1,0:T(8,128)S(1)}, u32[]{:S(2)}, u32[]{:S(2)}) collective-permute-start(f32[528,256]{1,0:T(8,128)S(1)} %get-tuple-element.25), channel_id=1, source_target_pairs={{12,8},{8,4},{4,0},{13,9},{9,5},{5,1},{14,10},{10,6},{6,2},{15,11}... | collective-permute-start | bytes 1622024 | tf_op jit(solution)/shard_map/ppermute | solution.py:376
  125.8 24.3 %collective-permute-start.10 = (f32[2,16,256]{2,1,0:T(8,128)S(1)}, f32[2,16,256]{2,1,0:T(8,128)S(1)}, u32[]{:S(2)}, u32[]{:S(2)}) collective-permute-start(f32[2,16,256]{2,1,0:T(8,128)S(1)} %gains.2), channel_id=1, source_target_pairs={{0,4},{4,8},{8,12},{12,0},{1,5},{5,9},{9,13},{13,1},{2,6},{6,10},{... | collective-permute-start | bytes 98312 | tf_op jit(solution)/shard_map/ppermute | solution.py:389
  132.9 17.8 %collective-permute-start.8 = (f32[2,16,256]{2,1,0:T(8,128)S(1)}, f32[2,16,256]{2,1,0:T(8,128)S(1)}, u32[]{:S(2)}, u32[]{:S(2)}) collective-permute-start(f32[2,16,256]{2,1,0:T(8,128)S(1)} %gains.2), channel_id=1, source_target_pairs={{0,12},{4,0},{8,4},{12,8},{1,13},{5,1},{9,5},{13,9},{2,14},{6,2},{... | collective-permute-start | bytes 98312 | tf_op jit(solution)/shard_map/ppermute | solution.py:389
  133.0 17.8 %collective-permute-start.9 = (f32[2,16,256]{2,1,0:T(8,128)S(1)}, f32[2,16,256]{2,1,0:T(8,128)S(1)}, u32[]{:S(2)}, u32[]{:S(2)}) collective-permute-start(f32[2,16,256]{2,1,0:T(8,128)S(1)} %gains.2), channel_id=1, source_target_pairs={{0,8},{4,12},{8,0},{12,4},{1,9},{5,13},{9,1},{13,5},{2,10},{6,14},... | collective-permute-start | bytes 98312 | tf_op jit(solution)/shard_map/ppermute | solution.py:389
  147.2 4.5 %collective-permute-start.18 = (f32[2,16,256]{2,1,0:T(8,128)S(1)}, f32[2,16,256]{2,1,0:T(8,128)S(1)}, u32[]{:S(2)}, u32[]{:S(2)}) collective-permute-start(f32[2,16,256]{2,1,0:T(8,128)S(1)} %gains.3), channel_id=1, source_target_pairs={{0,12},{4,0},{8,4},{12,8},{1,13},{5,1},{9,5},{13,9},{2,14},{6,2},{... | collective-permute-start | bytes 98312 | tf_op jit(solution)/shard_map/ppermute | solution.py:389
  150.1 4.8 %collective-permute-start.19 = (f32[2,16,256]{2,1,0:T(8,128)S(1)}, f32[2,16,256]{2,1,0:T(8,128)S(1)}, u32[]{:S(2)}, u32[]{:S(2)}) collective-permute-start(f32[2,16,256]{2,1,0:T(8,128)S(1)} %gains.3), channel_id=1, source_target_pairs={{0,8},{4,12},{8,0},{12,4},{1,9},{5,13},{9,1},{13,5},{2,10},{6,14},... | collective-permute-start | bytes 98312 | tf_op jit(solution)/shard_map/ppermute | solution.py:389
  150.1 5.7 %collective-permute-start.20 = (f32[2,16,256]{2,1,0:T(8,128)S(1)}, f32[2,16,256]{2,1,0:T(8,128)S(1)}, u32[]{:S(2)}, u32[]{:S(2)}) collective-permute-start(f32[2,16,256]{2,1,0:T(8,128)S(1)} %gains.3), channel_id=1, source_target_pairs={{0,4},{4,8},{8,12},{12,0},{1,5},{5,9},{9,13},{13,1},{2,6},{6,10},{... | collective-permute-start | bytes 98312 | tf_op jit(solution)/shard_map/ppermute | solution.py:389
  150.8 5.1 %collective-permute-start.11 = (f32[2,16,256]{2,1,0:T(8,128)S(1)}, f32[2,16,256]{2,1,0:T(8,128)S(1)}, u32[]{:S(2)}, u32[]{:S(2)}) collective-permute-start(f32[2,16,256]{2,1,0:T(8,128)S(1)} %select_select_fusion.2), channel_id=1, source_target_pairs={{0,1},{1,0},{2,3},{3,2},{4,5},{5,4},{6,7},{7,6},{8,9},{9,8},{10,11... | collective-permute-start | bytes 98312 | tf_op jit(solution)/shard_map/ppermute | solution.py:398
  155.9 1.3 collective-permute-start.21
  (9 other events, 34.4 us)

commit v2 on v1

--- a/solution.py
+++ b/solution.py
@@ -9,6 +9,8 @@
 
 reg_lambda = 1.0
 CHUNKS = 2
+LOW_SCALE = 16.0
+F8 = jnp.float8_e4m3fn
 TILE = 256
 MIB = 1024 * 1024
 VMEM_SPEC = pl.BlockSpec(memory_space=pltpu.VMEM)
@@ -29,7 +31,7 @@
     return roles
 
 
-def prep_kernel(line, slab, place_ref, owner_ref, bins_ref, grads_ref, hess_ref, side_ref, own_ref, send_ref, wt_ref, wt_send_ref, perm_ref):
+def prep_kernel(line, slab, place_ref, owner_ref, bins_ref, grads_ref, hess_ref, side_ref, own_ref, send_ref, wt_ref, undo_ref, wt_send_ref, perm_ref):
     f_dev = bins_ref.shape[1]
     half = f_dev // 2
     kdim = grads_ref.shape[1]
@@ -54,20 +56,54 @@
         rows = lax.broadcasted_iota(jnp.int32, (f_dev, f_dev), 0)
         perm_ref[...] = jnp.where(rows == source, 1.0, 0.0).astype(jnp.bfloat16)
 
+        eye_r = lax.broadcasted_iota(jnp.int32, (kdim, kdim), 0)
+        eye_c = lax.broadcasted_iota(jnp.int32, (kdim, kdim), 1)
+        eye = jnp.where(eye_r == eye_c, 1.0, 0.0).astype(jnp.bfloat16)
+        grads_t = lax.dot_general(eye, grads_ref[...], (((1,), (1,)), ((), ())), preferred_element_type=jnp.float32)
+        hess_row = jnp.broadcast_to(hess_ref[...].astype(jnp.float32), (8, hess_ref.shape[1]))
+        first = lax.broadcasted_iota(jnp.int32, hess_row.shape, 0) == 0
+        stacked = jnp.concatenate([grads_t, jnp.where(first, hess_row, 0.0)], axis=0)
+        masked = jnp.where(side_ref[...] == 1, stacked, 0.0)
+        wt_send_ref[...] = masked
+        wt_ref[...], undo_ref[...] = split_weights(masked)
+
     binned = bins_ref[...].astype(jnp.float32).astype(jnp.bfloat16)
     moved = jnp.dot(binned, perm_ref[...], preferred_element_type=jnp.float32)
     own_ref[...] = moved[:, :half].astype(jnp.bfloat16)
     send_ref[...] = moved[:, half:]
-    eye_r = lax.broadcasted_iota(jnp.int32, (kdim, kdim), 0)
-    eye_c = lax.broadcasted_iota(jnp.int32, (kdim, kdim), 1)
-    eye = jnp.where(eye_r == eye_c, 1.0, 0.0).astype(jnp.bfloat16)
-    grads_t = lax.dot_general(eye, grads_ref[...], (((1,), (1,)), ((), ())), preferred_element_type=jnp.float32)
-    hess_row = jnp.broadcast_to(hess_ref[...].astype(jnp.float32), (8, hess_ref.shape[1]))
-    first = lax.broadcasted_iota(jnp.int32, hess_row.shape, 0) == 0
-    stacked = jnp.concatenate([grads_t, jnp.where(first, hess_row, 0.0)], axis=0)
-    masked = jnp.where(side_ref[...] == 1, stacked, 0.0)
-    wt_send_ref[...] = masked
-    wt_ref[...] = jnp.concatenate([masked, jnp.zeros((8, masked.shape[1]), jnp.float32)], axis=0).astype(jnp.bfloat16)
+
+
+def split_weights(masked):
+    kdim = masked.shape[0] - 8
+    largest = jnp.max(jnp.abs(masked), axis=1, keepdims=True)
+    scale = jnp.full(largest.shape, 32.0, jnp.float32)
+    undo = jnp.full(largest.shape, 1.0 / 32.0, jnp.float32)
+    for e in (32, 16, 8, 4, 2, 1):
+        fits = largest * (scale * 2.0**e) < 256.0
+        scale = jnp.where(fits, scale * 2.0**e, scale)
+        undo = jnp.where(fits, undo * 2.0**-e, undo)
+    scaled = masked * scale
+    high = scaled.astype(F8).astype(jnp.float32)
+    low = (scaled - high) * LOW_SCALE
+    rest = jnp.zeros((16, masked.shape[1]), jnp.float32)
+    parts = jnp.concatenate([high[:kdim], low[:kdim], high[kdim:], low[kdim:], rest], axis=0)
+    return parts.astype(F8), jnp.broadcast_to(undo, (kdim + 8, 128))
+
+
+def split_kernel(masked_ref, wt_ref, undo_ref):
+    wt_ref[...], undo_ref[...] = split_weights(masked_ref[...])
+
+
+def split(masked):
+    height, rows = masked.shape
+    return pl.pallas_call(
+        split_kernel,
+        in_specs=[VMEM_SPEC],
+        out_specs=[VMEM_SPEC] * 2,
+        out_shape=[jax.ShapeDtypeStruct((2 * height + 16, rows), F8), jax.ShapeDtypeStruct((height, 128), jnp.float32)],
+        cost_estimate=pl.CostEstimate(flops=20 * height * rows, bytes_accessed=6 * height * rows, transcendentals=0),
+        name="split",
+    )(masked)
 
 
 def prep(line, slab, place, owners, bins, grads, hess, side):
@@ -82,71 +118,70 @@
             SMEM_SPEC,
             SMEM_SPEC,
             pl.BlockSpec((block, f_dev), lambda i: (i, 0)),
-            pl.BlockSpec((block, kdim), lambda i: (i, 0)),
-            pl.BlockSpec((1, block), lambda i: (0, i)),
-            pl.BlockSpec((1, block), lambda i: (0, i)),
+            pl.BlockSpec((rows, kdim), lambda i: (0, 0)),
+            pl.BlockSpec((1, rows), lambda i: (0, 0)),
+            pl.BlockSpec((1, rows), lambda i: (0, 0)),
         ],
         out_specs=[
             pl.BlockSpec((block, half), lambda i: (i, 0)),
             pl.BlockSpec((block, half), lambda i: (i, 0)),
-            pl.BlockSpec((kdim + 16, block), lambda i: (0, i)),
-            pl.BlockSpec((kdim + 8, block), lambda i: (0, i)),
+            pl.BlockSpec((2 * kdim + 32, rows), lambda i: (0, 0)),
+            pl.BlockSpec((kdim + 8, 128), lambda i: (0, 0)),
+            pl.BlockSpec((kdim + 8, rows), lambda i: (0, 0)),
         ],
         out_shape=[
             jax.ShapeDtypeStruct((rows, half), jnp.bfloat16),
             jax.ShapeDtypeStruct((rows, half), jnp.float32),
-            jax.ShapeDtypeStruct((kdim + 16, rows), jnp.bfloat16),
+            jax.ShapeDtypeStruct((2 * kdim + 32, rows), F8),
+            jax.ShapeDtypeStruct((kdim + 8, 128), jnp.float32),
             jax.ShapeDtypeStruct((kdim + 8, rows), jnp.float32),
         ],
         scratch_shapes=[pltpu.VMEM((f_dev, f_dev), jnp.bfloat16)],
-        compiler_params=pltpu.CompilerParams(vmem_limit_bytes=24 * MIB),
+        compiler_params=pltpu.CompilerParams(vmem_limit_bytes=56 * MIB),
         cost_estimate=pl.CostEstimate(flops=2 * rows * f_dev * f_dev, bytes_accessed=8 * rows * f_dev, transcendentals=0),
         name="prep",
     )(place, owners, bins, grads, hess, side)
 
 
 def hist_kernel(first_column, width, levels, parts, kdim, has_init, *refs):
-    refs = list(refs)
-    lanes = refs[-3].shape[1]
-    pairs = [(refs[2 * i], refs[2 * i + 1]) for i in range(parts)]
-    init_ref = refs[2 * parts] if has_init else None
-    out_ref, rel_ref, wt_ref = refs[-3:]
-    half = pairs[0][0].shape[1]
-    rows = pairs[0][0].shape[0]
+    parts_in = [refs[3 * i : 3 * i + 3] for i in range(parts)]
+    init_ref = refs[3 * parts] if has_init else None
+    out_ref, rel_ref = refs[-2:]
+    lanes = out_ref.shape[1]
+    rows, half = parts_in[0][0].shape
     src = lax.broadcasted_iota(jnp.int32, (half, lanes), 0)
     dst = lax.broadcasted_iota(jnp.int32, (half, lanes), 1)
     spread = jnp.where(src == first_column + lax.rem(dst, width), 1.0, 0.0).astype(jnp.bfloat16)
     lane = lax.broadcasted_iota(jnp.int32, (1, lanes), 1)
     shift = ((lane // width) * levels).astype(jnp.float32)
-    for i, (bins_ref, w_ref) in enumerate(pairs):
+    for i, (bins_ref, _, _) in enumerate(parts_in):
         for r in range(0, rows, TILE):
             block = bins_ref[r : r + TILE, :].astype(jnp.bfloat16)
             moved = jnp.dot(block, spread, preferred_element_type=jnp.float32)
             rel_ref[i * rows + r : i * rows + r + TILE, :] = (moved - shift).astype(jnp.bfloat16)
-        if w_ref.dtype == jnp.bfloat16:
-            wt_ref[:, i * rows : (i + 1) * rows] = w_ref[...]
-        else:
-            part = jnp.concatenate([w_ref[...], jnp.zeros((8, rows), jnp.float32)], axis=0)
-            wt_ref[:, i * rows : (i + 1) * rows] = part.astype(jnp.bfloat16)
-    tiles = parts * rows // TILE
     one = jnp.ones((TILE, lanes), jnp.bfloat16)
     zero = jnp.zeros((TILE, lanes), jnp.bfloat16)
 
     def level(b, carry):
         value = jnp.full((TILE, lanes), b.astype(jnp.float32), jnp.float32).astype(jnp.bfloat16)
-        total = jnp.zeros((wt_ref.shape[0], lanes), jnp.float32)
-        for t in range(tiles):
-            hit = rel_ref[t * TILE : (t + 1) * TILE, :] == value
-            onehot = jnp.where(hit, one, zero)
-            total = total + jnp.dot(wt_ref[:, t * TILE : (t + 1) * TILE], onehot, preferred_element_type=jnp.float32)
         start = pl.multiple_of(b * kdim, kdim)
-        grad = total[:kdim, :]
-        hess = total[kdim : kdim + 1, :]
+        hess_at = levels * kdim + b
         if has_init:
-            grad = grad + init_ref[pl.ds(start, kdim), :]
-            hess = hess + init_ref[pl.ds(levels * kdim + b, 1), :]
+            grad, hess = init_ref[pl.ds(start, kdim), :], init_ref[pl.ds(hess_at, 1), :]
+        else:
+            grad, hess = jnp.zeros((kdim, lanes), jnp.float32), jnp.zeros((1, lanes), jnp.float32)
+        for i, (_, wt_ref, undo_ref) in enumerate(parts_in):
+            total = jnp.zeros((wt_ref.shape[0], lanes), jnp.float32)
+            for r in range(0, rows, TILE):
+                hit = rel_ref[i * rows + r : i * rows + r + TILE, :] == value
+                onehot = jnp.where(hit, one, zero).astype(F8)
+                total = total + jnp.dot(wt_ref[:, r : r + TILE], onehot, preferred_element_type=jnp.float32)
+            grad_part = total[:kdim] + total[kdim : 2 * kdim] * (1.0 / LOW_SCALE)
+            hess_part = total[2 * kdim : 2 * kdim + 1] + total[2 * kdim + 8 : 2 * kdim + 9] * (1.0 / LOW_SCALE)
+            grad = grad + grad_part * undo_ref[:kdim, :1]
+            hess = hess + hess_part * undo_ref[kdim : kdim + 1, :1]
         out_ref[pl.ds(start, kdim), :] = grad
-        out_ref[pl.ds(levels * kdim + b, 1), :] = hess
+        out_ref[pl.ds(hess_at, 1), :] = hess
         return carry
 
     lax.fori_loop(0, levels, level, 0)
@@ -164,10 +199,7 @@
         in_specs=[VMEM_SPEC] * len(operands),
         out_specs=VMEM_SPEC,
         out_shape=jax.ShapeDtypeStruct((height, lanes), jnp.float32),
-        scratch_shapes=[
-            pltpu.VMEM((parts * rows, lanes), jnp.bfloat16),
-            pltpu.VMEM((kdim + 16, parts * rows), jnp.bfloat16),
-        ],
+        scratch_shapes=[pltpu.VMEM((parts * rows, lanes), jnp.bfloat16)],
         compiler_params=pltpu.CompilerParams(vmem_limit_bytes=24 * MIB),
         cost_estimate=pl.CostEstimate(
             flops=2 * 256 * parts * rows * levels * lanes, bytes_accessed=parts * rows * lanes * 4, transcendentals=0
@@ -325,18 +357,20 @@
     plan = plan_of(line)
 
     where = jnp.stack([z, core]).astype(jnp.int32)
-    own, send, wt, wt_send = prep(
+    own, send, wt, undo, wt_send = prep(
         line, slab, where, parent_owner, bins, grads, hess.reshape(1, rows), node_side.reshape(1, rows)
     )
     swap = [(0, 1), (1, 0)]
+    wt_other = lax.ppermute(wt_send, "sub", swap)
     other = lax.ppermute(send, "sub", swap)
-    wt_other = lax.ppermute(wt_send, "sub", swap)
+    mine = (own, wt, undo)
+    theirs = (other, *split(wt_other))
 
     units = {}
     for c in range(chunks):
-        units[0, c] = hist(c * width, width, levels, lanes, kdim, [(own, wt)])
+        units[0, c] = hist(c * width, width, levels, lanes, kdim, [mine])
     for c in range(chunks):
-        units[0, c] = hist(c * width, width, levels, lanes, kdim, [(other, wt_other)], units[0, c])
+        units[0, c] = hist(c * width, width, levels, lanes, kdim, [theirs], units[0, c])
 
     def pick(kind, step, c):
         where_at = {}
@@ -350,6 +384,36 @@
             value = jnp.where(one_of(z, where_at[p]), units[p, c], value)
         return value
 
+    from_left = [None] * chunks
+    from_right = [None] * chunks
+    arrived = {}
+
+    def after(step, c):
+        if (step, c) not in arrived:
+            return [mine, theirs]
+        held, _ = lax.optimization_barrier((own, arrived[step, c]))
+        return [(held, wt, undo), theirs]
+
+    for step in range(line - 1):
+        if step > 0:
+            for c in range(chunks):
+                units[step, c] = hist(step * slab + c * width, width, levels, lanes, kdim, after(step - 2, c))
+        for c in range(chunks):
+            to_right = pick("R", step, c)
+            to_left = pick("L", step, c)
+            if step > 0:
+                to_right = to_right + from_left[c]
+                to_left = to_left + from_right[c]
+            from_left[c] = lax.ppermute(to_right, "dp", [(i, i + 1) for i in range(step + 1)])
+            from_right[c] = lax.ppermute(to_left, "dp", [(line - 1 - i, line - 2 - i) for i in range(step + 1)])
+            arrived[step, c] = from_left[c]
+    last = line - 1
+    for c in range(chunks):
+        units[last, c] = hist(last * slab + c * width, width, levels, lanes, kdim, after(last - 2, c))
+
+    signs, child_owner, parent_owner, node_low, node_high, parent_grad, parent_hess, _ = lax.optimization_barrier(
+        (signs, child_owner, parent_owner, node_low, node_high, parent_grad, parent_hess, arrived[max(line - 3, 0), 0])
+    )
     slots = jnp.arange(owners, dtype=jnp.int32)
     parent_inv = inverse_of(parent_owner, slots)
     my_slab = parent_inv[place]
@@ -359,24 +423,6 @@
     bounds = jnp.stack([node_low, node_high])
     par_hess = jnp.transpose(parent_hess[0].reshape(chunks, width, groups, levels), (0, 3, 2, 1)).reshape(chunks, levels, lanes)
     par_grad = parent_layout(width, levels, lanes, kdim, chunks, parent_grad[0])
-
-    from_left = [None] * chunks
-    from_right = [None] * chunks
-    for step in range(line - 1):
-        if step > 0:
-            for c in range(chunks):
-                units[step, c] = hist(step * slab + c * width, width, levels, lanes, kdim, [(own, wt), (other, wt_other)])
-        for c in range(chunks):
-            to_right = pick("R", step, c)
-            to_left = pick("L", step, c)
-            if step > 0:
-                to_right = to_right + from_left[c]
-                to_left = to_left + from_right[c]
-            from_left[c] = lax.ppermute(to_right, "dp", [(i, i + 1) for i in range(step + 1)])
-            from_right[c] = lax.ppermute(to_left, "dp", [(line - 1 - i, line - 2 - i) for i in range(step + 1)])
-    last = line - 1
-    for c in range(chunks):
-        units[last, c] = hist(last * slab + c * width, width, levels, lanes, kdim, [(own, wt), (other, wt_other)])
 
     child_inv = inverse_of(child_owner, slots)
     source_of = jnp.sum(jnp.where(child_inv[:, None] == slots[None, :], parent_owner[None, :], 0), axis=1)

time: 159 us -> 144 us (0.906)
  Pallas kernels: 93.7 us -> 72.4 us
  other arithmetic: 1.1 us -> 5.97 us
  local copies, waits for them, and re-layouts: 10.7 us -> 15.2 us
  starting transfers between devices: 40.2 us -> 36.5 us
    pallas_call x10, Pallas kernels: 84.3 us -> 58.8 us  [hist(): pl.pallas_call(functools.partial(hist_kernel, first_column, width, levels...]
    add x4, other arithmetic: 0.57 us -> 4.93 us  [per_device(): to_left = to_left + from_right[c]]
    unnamed x24 -> x51, local copies, waits for them, and re-layouts: 6.43 us -> 10.2 us
    ppermute x6, starting transfers between devices: 12.2 us -> 8.88 us  [per_device(): lax.ppermute(gain, 'dp', [(i, (i + s) % line) for i in range(line)])]
    pallas_call x1, Pallas kernels: 3.77 us -> 6.03 us  [prep(): pl.pallas_call(functools.partial(prep_kernel, line, slab), grid=(rows //...]
    pallas_call x0 -> x1, Pallas kernels: none -> 1.9 us  [split(): pl.pallas_call(split_kernel, in_specs=[VMEM_SPEC], out_specs=[VMEM_SPEC]...]
  transfers between devices with their start and end apart: 22 -> 22, of which waited for: 5 -> 5; matrix products, arithmetic and copies ran while one was open for 2% -> 6% of each run, Pallas kernels for 53% -> 43%
where the time goes in v2:
time: 144 us; the launch traced here: 143 us
  Pallas kernels  72.4 us (50%)
  starting transfers between devices  36.5 us (25%)
  local copies, waits for them, and re-layouts  15.2 us (11%)
  between operations  6.71 us (5%)
  waiting for transfers between devices  6.55 us (5%)
  other arithmetic  5.97 us (4%)
    pallas_call x10, Pallas kernels, hist(): pl.pallas_call(functools.partial(hist_kernel, first_column, width, levels...  58.8 us
    ppermute x6, starting transfers between devices, per_device(): lax.ppermute(to_right, 'dp', [(i, i + 1) for i in range(step + 1)])  20.8 us
    unnamed x51, local copies, waits for them, and re-layouts  10.2 us
    ppermute x6, starting transfers between devices, per_device(): lax.ppermute(gain, 'dp', [(i, (i + s) % line) for i in range(line)])  8.88 us
    ppermute x6, starting transfers between devices, per_device(): lax.ppermute(to_left, 'dp', [(line - 1 - i, line - 2 - i) for i in range(...  6.14 us
    pallas_call x1, Pallas kernels, prep(): pl.pallas_call(functools.partial(prep_kernel, line, slab), grid=(rows //...  6.03 us
    pallas_call x2, Pallas kernels, gains_of(): pl.pallas_call(functools.partial(gain_kernel, width, levels, kdim), in_sp...  5.35 us
    add x4, other arithmetic, per_device(): to_left = to_left + from_right[c]  4.93 us
  transfers between devices with their start and end apart: 22, of which 5 were waited for; matrix products, arithmetic and copies ran while one was open for 6% of the time, Pallas kernels for 43%

profile of v2, /device:TPU:0, one launch (start us, length us, event | category | flops | bytes accessed | tf_op | source)
XLA Modules:
  0.0 143.3 jit_solution(4418405623289277216)
XLA Ops:
  0.0 1.9 %copy.23.grads_ref = bf16[2048,32]{1,0:T(8,128)(2,1)} copy(bf16[2048,32]{0,1:T(8,128)(2,1)} %param.12) | data formatting | bytes 262144 | tf_op args[1]
  3.8 6.0 %prep.1 = (bf16[2048,256]{1,0:T(8,128)(2,1)}, f32[2048,256]{1,0:T(8,128)}, f8e4m3fn[96,2048]{1,0:T(32,128)(4,1)}, f32[40,128]{1,0:T(8,128)}, f32[40,2048]{1,0:T(8,128)}) custom-call(s32[2]{0:T(128)} %pad_add_fusion.1.place_ref, s32[8]{0:T(128)} %owner_ref.1, s32[2048,512]{1,0:T(8,128)} %bins_ref.1, bf16[2048,32]{1,0:T(8,128)(2,1)} %copy.23.grads_ref, ...), custom_call_target="tpu_custom_call" | custom-call | flops 1073741824 | bytes 8388608 | tf_op jit(solution)/shard_map/prep/pallas_call | solution.py:114
  13.2 4.5 %hist.11.refs_3_ = f32[528,256]{1,0:T(8,128)S(1)} custom-call(bf16[2048,256]{1,0:T(8,128)(2,1)S(1)} %copy-done.7, f8e4m3fn[96,2048]{1,0:T(32,128)(4,1)S(1)} %copy-done.10, f32[40,128]{1,0:T(8,128)S(1)} %copy-done.15), custom_call_target="tpu_custom_call" | custom-call | flops 4294967296 | bytes 2097152 | tf_op jit(solution)/shard_map/hist/pallas_call | solution.py:197
  17.7 4.5 %hist.16.refs_3_ = f32[528,256]{1,0:T(8,128)S(1)} custom-call(bf16[2048,256]{1,0:T(8,128)(2,1)S(1)} %copy-done.7, f8e4m3fn[96,2048]{1,0:T(32,128)(4,1)S(1)} %copy-done.10, f32[40,128]{1,0:T(8,128)S(1)} %copy-done.15), custom_call_target="tpu_custom_call" | custom-call | flops 4294967296 | bytes 2097152 | tf_op jit(solution)/shard_map/hist/pallas_call | solution.py:197
  22.9 1.9 %split.1 = (f8e4m3fn[96,2048]{1,0:T(32,128)(4,1)}, f32[40,128]{1,0:T(8,128)}) custom-call(f32[40,2048]{1,0:T(8,128)} %copy-done.19), custom_call_target="tpu_custom_call" | custom-call | flops 1638400 | bytes 491520 | tf_op jit(solution)/shard_map/split/pallas_call | solution.py:99
  26.6 4.5 %hist.12 = f32[528,256]{1,0:T(8,128)S(1)} custom-call(f32[2048,256]{1,0:T(8,128)S(1)} %collective-permute-done.refs_3_.refs_0_, f8e4m3fn[96,2048]{1,0:T(32,128)(4,1)S(1)} %copy-done.12, f32[40,128]{1,0:T(8,128)S(1)} %copy-done.17, f32[528,256]{1,0:T(8,128)S(1)} %hist.11.refs_3_), custom_call_target="tpu_custom_call" | custom-call | flops 4294967296 | bytes 2097152 | tf_op jit(solution)/shard_map/hist/pallas_call | solution.py:197
  31.2 5.1 %collective-permute-start.2 = (f32[528,256]{1,0:T(8,128)S(1)}, f32[528,256]{1,0:T(8,128)S(1)}, u32[]{:S(2)}, u32[]{:S(2)}) collective-permute-start(f32[528,256]{1,0:T(8,128)S(1)} %hist.12), channel_id=1, source_target_pairs={{0,4},{1,5},{2,6},{3,7},{16,20},{17,21},{18,22},{19,23}} | collective-permute-start | bytes 1622024 | tf_op jit(solution)/shard_map/ppermute | solution.py:407
  37.0 4.5 %hist.17 = f32[528,256]{1,0:T(8,128)S(1)} custom-call(f32[2048,256]{1,0:T(8,128)S(1)} %collective-permute-done.refs_3_.refs_0_, f8e4m3fn[96,2048]{1,0:T(32,128)(4,1)S(1)} %copy-done.12, f32[40,128]{1,0:T(8,128)S(1)} %copy-done.17, f32[528,256]{1,0:T(8,128)S(1)} %hist.16.refs_3_), custom_call_target="tpu_custom_call" | custom-call | flops 4294967296 | bytes 2097152 | tf_op jit(solution)/shard_map/hist/pallas_call | solution.py:197
  43.6 6.8 %hist.10 = f32[528,256]{1,0:T(8,128)S(1)} custom-call(bf16[2048,256]{1,0:T(8,128)(2,1)S(1)} %copy-done.8, f8e4m3fn[96,2048]{1,0:T(32,128)(4,1)S(1)} %copy-done.11, f32[40,128]{1,0:T(8,128)S(1)} %copy-done.16, f32[2048,256]{1,0:T(8,128)S(1)} %collective-permute-done.refs_3_.refs_0_, f8e4m3fn[96,2048]{1,0:T(32,128)(4,1)S(1)} %copy-done.12, ...), custom_call_target="tpu_custom_call" | custom-call | flops 8589934592 | bytes 4194304 | tf_op jit(solution)/shard_map/hist/pallas_call | solution.py:197
  50.4 6.8 %hist.15 = f32[528,256]{1,0:T(8,128)S(1)} custom-call(bf16[2048,256]{1,0:T(8,128)(2,1)S(1)} %copy-done.8, f8e4m3fn[96,2048]{1,0:T(32,128)(4,1)S(1)} %copy-done.11, f32[40,128]{1,0:T(8,128)S(1)} %copy-done.16, f32[2048,256]{1,0:T(8,128)S(1)} %collective-permute-done.refs_3_.refs_0_, f8e4m3fn[96,2048]{1,0:T(32,128)(4,1)S(1)} %copy-done.12, ...), custom_call_target="tpu_custom_call" | custom-call | flops 8589934592 | bytes 4194304 | tf_op jit(solution)/shard_map/hist/pallas_call | solution.py:197
  61.4 5.2 %collective-permute-start.13 = (f32[528,256]{1,0:T(8,128)}, f32[528,256]{1,0:T(8,128)}, u32[]{:S(2)}, u32[]{:S(2)}) collective-permute-start(f32[528,256]{1,0:T(8,128)} %get-tuple-element.50), channel_id=1, source_target_pairs={{0,4},{4,8},{1,5},{5,9},{2,6},{6,10},{3,7},{7,11},{16,20},{20,24},... | collective-permute-start | bytes 1622024 | tf_op jit(solution)/shard_map/ppermute | solution.py:407
  68.1 6.8 %hist.14 = f32[528,256]{1,0:T(8,128)S(1)} custom-call(bf16[2048,256]{1,0:T(8,128)(2,1)S(1)} %copy-done.8, f8e4m3fn[96,2048]{1,0:T(32,128)(4,1)S(1)} %copy-done.11, f32[40,128]{1,0:T(8,128)S(1)} %copy-done.16, f32[2048,256]{1,0:T(8,128)S(1)} %collective-permute-done.refs_3_.refs_0_, f8e4m3fn[96,2048]{1,0:T(32,128)(4,1)S(1)} %copy-done.12, ...), custom_call_target="tpu_custom_call" | custom-call | flops 8589934592 | bytes 4194304 | tf_op jit(solution)/shard_map/hist/pallas_call | solution.py:197
  74.9 6.8 %hist.19 = f32[528,256]{1,0:T(8,128)S(1)} custom-call(bf16[2048,256]{1,0:T(8,128)(2,1)S(1)} %copy-done.8, f8e4m3fn[96,2048]{1,0:T(32,128)(4,1)S(1)} %copy-done.11, f32[40,128]{1,0:T(8,128)S(1)} %copy-done.16, f32[2048,256]{1,0:T(8,128)S(1)} %collective-permute-done.refs_3_.refs_0_, f8e4m3fn[96,2048]{1,0:T(32,128)(4,1)S(1)} %copy-done.12, ...), custom_call_target="tpu_custom_call" | custom-call | flops 8589934592 | bytes 4194304 | tf_op jit(solution)/shard_map/hist/pallas_call | solution.py:197
  83.0 2.7 %collective-permute-start.4 = (f32[528,256]{1,0:T(8,128)}, f32[528,256]{1,0:T(8,128)S(1)}, u32[]{:S(2)}, u32[]{:S(2)}) collective-permute-start(f32[528,256]{1,0:T(8,128)} %get-tuple-element.52), channel_id=1, source_target_pairs={{0,4},{4,8},{8,12},{1,5},{5,9},{9,13},{2,6},{6,10},{10,14},{3,7},{... | collective-permute-start | bytes 1622024 | tf_op jit(solution)/shard_map/ppermute | solution.py:407
  91.9 2.5 %fusion.1 = (f32[528,256]{1,0:T(8,128)}, f32[528,256]{1,0:T(8,128)}) fusion(f32[528,256]{1,0:T(8,128)S(1)} %hist.19, f32[528,256]{1,0:T(8,128)} %collective-permute-done.16, f32[528,256]{1,0:T(8,128)} %collective-permute-done.13, f32[528,256]{1,0:T(8,128)S(1)} %hist.15, pred[]{:T(512)S(6)} %eq.32), kind=kLoop, calls=%fused_computation.20 | loop fusion | flops 405504 | bytes 3244033 | tf_op jit(solution)/shard_map/add | solution.py:406
  94.4 5.2 %collective-permute-start.14 = (f32[528,256]{1,0:T(8,128)}, f32[528,256]{1,0:T(8,128)S(1)}, u32[]{:S(2)}, u32[]{:S(2)}) collective-permute-start(f32[528,256]{1,0:T(8,128)} %get-tuple-element.54), channel_id=1, source_target_pairs={{0,4},{4,8},{8,12},{1,5},{5,9},{9,13},{2,6},{6,10},{10,14},{3,7},{... | collective-permute-start | bytes 1622024 | tf_op jit(solution)/shard_map/ppermute | solution.py:407
  102.1 6.8 %hist.13.last_ref = f32[528,256]{1,0:T(8,128)S(1)} custom-call(bf16[2048,256]{1,0:T(8,128)(2,1)S(1)} %copy-done.9, f8e4m3fn[96,2048]{1,0:T(32,128)(4,1)S(1)} %copy-done.11, f32[40,128]{1,0:T(8,128)S(1)} %copy-done.16, f32[2048,256]{1,0:T(8,128)S(1)} %copy-done.6, f8e4m3fn[96,2048]{1,0:T(32,128)(4,1)S(1)} %copy-done.13, f32[40,128]{1,0:T(8,128)S(1)} %copy-done.18), custom_call_target="tpu_custom_call" | custom-call | flops 8589934592 | bytes 4194304 | tf_op jit(solution)/shard_map/hist/pallas_call | solution.py:197
  109.0 2.7 %gains.2 = f32[2,16,256]{2,1,0:T(8,128)S(1)} custom-call(f32[528,256]{1,0:T(8,128)S(1)} %hist.13.last_ref, f32[528,256]{1,0:T(8,128)S(1)} %collective-permute-done.4.right_ref, f32[528,256]{1,0:T(8,128)S(1)} %collective-permute-done.7.left_ref, f32[512,256]{1,0:T(8,128)S(1)} %copy-done.4, f32[16,256]{1,0:T(8,128)S(1)} %squeeze.20.par_hess_ref, ...), custom_call_target="tpu_custom_call" | custom-call | flops 6553600 | bytes 2097152 | tf_op jit(solution)/shard_map/gains/pallas_call | solution.py:315
  111.7 2.7 %collective-permute-start.10 = (f32[2,16,256]{2,1,0:T(8,128)S(1)}, f32[2,16,256]{2,1,0:T(8,128)S(1)}, u32[]{:S(2)}, u32[]{:S(2)}) collective-permute-start(f32[2,16,256]{2,1,0:T(8,128)S(1)} %gains.2), channel_id=1, source_target_pairs={{0,4},{4,8},{8,12},{12,0},{1,5},{5,9},{9,13},{13,1},{2,6},{6,10},{... | collective-permute-start | bytes 98312 | tf_op jit(solution)/shard_map/ppermute | solution.py:435
  115.5 2.3 %collective-permute-start.9 = (f32[2,16,256]{2,1,0:T(8,128)S(1)}, f32[2,16,256]{2,1,0:T(8,128)S(1)}, u32[]{:S(2)}, u32[]{:S(2)}) collective-permute-start(f32[2,16,256]{2,1,0:T(8,128)S(1)} %gains.2), channel_id=1, source_target_pairs={{0,8},{4,12},{8,0},{12,4},{1,9},{5,13},{9,1},{13,5},{2,10},{6,14},... | collective-permute-start | bytes 98312 | tf_op jit(solution)/shard_map/ppermute | solution.py:435
  117.8 6.8 %hist.18.last_ref = f32[528,256]{1,0:T(8,128)S(1)} custom-call(bf16[2048,256]{1,0:T(8,128)(2,1)S(1)} %copy-done.9, f8e4m3fn[96,2048]{1,0:T(32,128)(4,1)S(1)} %copy-done.11, f32[40,128]{1,0:T(8,128)S(1)} %copy-done.16, f32[2048,256]{1,0:T(8,128)S(1)} %copy-done.6, f8e4m3fn[96,2048]{1,0:T(32,128)(4,1)S(1)} %copy-done.14, f32[40,128]{1,0:T(8,128)S(1)} %copy-done.18), custom_call_target="tpu_custom_call" | custom-call | flops 8589934592 | bytes 4194304 | tf_op jit(solution)/shard_map/hist/pallas_call | solution.py:197
  130.9 2.7 %gains.3 = f32[2,16,256]{2,1,0:T(8,128)S(1)} custom-call(f32[528,256]{1,0:T(8,128)S(1)} %hist.18.last_ref, f32[528,256]{1,0:T(8,128)S(1)} %collective-permute-done.14.right_ref, f32[528,256]{1,0:T(8,128)S(1)} %collective-permute-done.17.left_ref, f32[512,256]{1,0:T(8,128)S(1)} %copy-done.2, f32[16,256]{1,0:T(8,128)S(1)} %squeeze.22.par_hess_ref, ...), custom_call_target="tpu_custom_call" | custom-call | flops 6553600 | bytes 2097152 | tf_op jit(solution)/shard_map/gains/pallas_call | solution.py:315
  137.6 1.8 %collective-permute-done.19 = f32[2,16,256]{2,1,0:T(8,128)S(1)} collective-permute-done((f32[2,16,256]{2,1,0:T(8,128)S(1)}, f32[2,16,256]{2,1,0:T(8,128)S(1)}, u32[]{:S(2)}, u32[]{:S(2)}) %collective-permute-start.19) | collective-permute-done | bytes 32800 | tf_op jit(solution)/shard_map/ppermute | solution.py:435
  139.4 1.7 %collective-permute-done.20 = f32[2,16,256]{2,1,0:T(8,128)S(1)} collective-permute-done((f32[2,16,256]{2,1,0:T(8,128)S(1)}, f32[2,16,256]{2,1,0:T(8,128)S(1)}, u32[]{:S(2)}, u32[]{:S(2)}) %collective-permute-start.20) | collective-permute-done | bytes 32800 | tf_op jit(solution)/shard_map/ppermute | solution.py:435
  (120 shorter events, 33.5 us)
Async XLA Ops:
  9.8 15.0 %collective-permute-start = (f32[2048,256]{1,0:T(8,128)}, f32[2048,256]{1,0:T(8,128)S(1)}, u32[]{:S(2)}, u32[]{:S(2)}) collective-permute-start(f32[2048,256]{1,0:T(8,128)} %get-tuple-element.28), channel_id=1, source_target_pairs={{0,1},{1,0},{2,3},{3,2},{4,5},{5,4},{6,7},{7,6},{8,9},{9,8},{10,11... | collective-permute-start | bytes 6291464 | tf_op jit(solution)/shard_map/ppermute | solution.py:365
  10.3 11.9 %collective-permute-start.1 = (f32[40,2048]{1,0:T(8,128)}, f32[40,2048]{1,0:T(8,128)S(1)}, u32[]{:S(2)}, u32[]{:S(2)}) collective-permute-start(f32[40,2048]{1,0:T(8,128)} %get-tuple-element.29), channel_id=1, source_target_pairs={{0,1},{1,0},{2,3},{3,2},{4,5},{5,4},{6,7},{7,6},{8,9},{9,8},{10,11... | collective-permute-start | bytes 983048 | tf_op jit(solution)/shard_map/ppermute | solution.py:364
  24.8 50.1 %copy-start.5 = (f32[2048,256]{1,0:T(8,128)}, f32[2048,256]{1,0:T(8,128)S(1)}, u32[]{:S(2)}) copy-start(f32[2048,256]{1,0:T(8,128)S(1)} %collective-permute-done.refs_3_.refs_0_) | copy-start | bytes 6291460
  31.2 26.0 %collective-permute-start.2 = (f32[528,256]{1,0:T(8,128)S(1)}, f32[528,256]{1,0:T(8,128)S(1)}, u32[]{:S(2)}, u32[]{:S(2)}) collective-permute-start(f32[528,256]{1,0:T(8,128)S(1)} %hist.12), channel_id=1, source_target_pairs={{0,4},{1,5},{2,6},{3,7},{16,20},{17,21},{18,22},{19,23}} | collective-permute-start | bytes 1622024 | tf_op jit(solution)/shard_map/ppermute | solution.py:407
  36.3 20.9 %collective-permute-start.5 = (f32[528,256]{1,0:T(8,128)S(1)}, f32[528,256]{1,0:T(8,128)S(1)}, u32[]{:S(2)}, u32[]{:S(2)}) collective-permute-start(f32[528,256]{1,0:T(8,128)S(1)} %hist.12), channel_id=1, source_target_pairs={{12,8},{13,9},{14,10},{15,11},{28,24},{29,25},{30,26},{31,27}} | collective-permute-start | bytes 1622024 | tf_op jit(solution)/shard_map/ppermute | solution.py:408
  41.6 18.7 %collective-permute-start.12 = (f32[528,256]{1,0:T(8,128)S(1)}, f32[528,256]{1,0:T(8,128)S(1)}, u32[]{:S(2)}, u32[]{:S(2)}) collective-permute-start(f32[528,256]{1,0:T(8,128)S(1)} %hist.17), channel_id=1, source_target_pairs={{0,4},{1,5},{2,6},{3,7},{16,20},{17,21},{18,22},{19,23}} | collective-permute-start | bytes 1622024 | tf_op jit(solution)/shard_map/ppermute | solution.py:407
  42.9 17.4 %collective-permute-start.15 = (f32[528,256]{1,0:T(8,128)S(1)}, f32[528,256]{1,0:T(8,128)S(1)}, u32[]{:S(2)}, u32[]{:S(2)}) collective-permute-start(f32[528,256]{1,0:T(8,128)S(1)} %hist.17), channel_id=1, source_target_pairs={{12,8},{13,9},{14,10},{15,11},{28,24},{29,25},{30,26},{31,27}} | collective-permute-start | bytes 1622024 | tf_op jit(solution)/shard_map/ppermute | solution.py:408
  57.4 24.4 %collective-permute-start.3 = (f32[528,256]{1,0:T(8,128)S(1)}, f32[528,256]{1,0:T(8,128)S(1)}, u32[]{:S(2)}, u32[]{:S(2)}) collective-permute-start(f32[528,256]{1,0:T(8,128)S(1)} %get-tuple-element.48), channel_id=1, source_target_pairs={{0,4},{4,8},{1,5},{5,9},{2,6},{6,10},{3,7},{7,11},{16,20},{20,24},... | collective-permute-start | bytes 1622024 | tf_op jit(solution)/shard_map/ppermute | solution.py:407
  58.7 23.0 %collective-permute-start.6 = (f32[528,256]{1,0:T(8,128)S(1)}, f32[528,256]{1,0:T(8,128)S(1)}, u32[]{:S(2)}, u32[]{:S(2)}) collective-permute-start(f32[528,256]{1,0:T(8,128)S(1)} %get-tuple-element.47), channel_id=1, source_target_pairs={{12,8},{8,4},{13,9},{9,5},{14,10},{10,6},{15,11},{11,7},{28,24},{2... | collective-permute-start | bytes 1622024 | tf_op jit(solution)/shard_map/ppermute | solution.py:408
  61.4 30.4 %collective-permute-start.13 = (f32[528,256]{1,0:T(8,128)}, f32[528,256]{1,0:T(8,128)}, u32[]{:S(2)}, u32[]{:S(2)}) collective-permute-start(f32[528,256]{1,0:T(8,128)} %get-tuple-element.50), channel_id=1, source_target_pairs={{0,4},{4,8},{1,5},{5,9},{2,6},{6,10},{3,7},{7,11},{16,20},{20,24},... | collective-permute-start | bytes 1622024 | tf_op jit(solution)/shard_map/ppermute | solution.py:407
  66.6 25.3 %collective-permute-start.16 = (f32[528,256]{1,0:T(8,128)}, f32[528,256]{1,0:T(8,128)}, u32[]{:S(2)}, u32[]{:S(2)}) collective-permute-start(f32[528,256]{1,0:T(8,128)} %get-tuple-element.49), channel_id=1, source_target_pairs={{12,8},{8,4},{13,9},{9,5},{14,10},{10,6},{15,11},{11,7},{28,24},{2... | collective-permute-start | bytes 1622024 | tf_op jit(solution)/shard_map/ppermute | solution.py:408
  83.0 26.0 %collective-permute-start.4 = (f32[528,256]{1,0:T(8,128)}, f32[528,256]{1,0:T(8,128)S(1)}, u32[]{:S(2)}, u32[]{:S(2)}) collective-permute-start(f32[528,256]{1,0:T(8,128)} %get-tuple-element.52), channel_id=1, source_target_pairs={{0,4},{4,8},{8,12},{1,5},{5,9},{9,13},{2,6},{6,10},{10,14},{3,7},{... | collective-permute-start | bytes 1622024 | tf_op jit(solution)/shard_map/ppermute | solution.py:407
  85.7 23.3 %collective-permute-start.7 = (f32[528,256]{1,0:T(8,128)}, f32[528,256]{1,0:T(8,128)S(1)}, u32[]{:S(2)}, u32[]{:S(2)}) collective-permute-start(f32[528,256]{1,0:T(8,128)} %get-tuple-element.51), channel_id=1, source_target_pairs={{12,8},{8,4},{4,0},{13,9},{9,5},{5,1},{14,10},{10,6},{6,2},{15,11}... | collective-permute-start | bytes 1622024 | tf_op jit(solution)/shard_map/ppermute | solution.py:408
  94.4 36.6 %collective-permute-start.14 = (f32[528,256]{1,0:T(8,128)}, f32[528,256]{1,0:T(8,128)S(1)}, u32[]{:S(2)}, u32[]{:S(2)}) collective-permute-start(f32[528,256]{1,0:T(8,128)} %get-tuple-element.54), channel_id=1, source_target_pairs={{0,4},{4,8},{8,12},{1,5},{5,9},{9,13},{2,6},{6,10},{10,14},{3,7},{... | collective-permute-start | bytes 1622024 | tf_op jit(solution)/shard_map/ppermute | solution.py:407
  99.5 31.4 %collective-permute-start.17 = (f32[528,256]{1,0:T(8,128)}, f32[528,256]{1,0:T(8,128)S(1)}, u32[]{:S(2)}, u32[]{:S(2)}) collective-permute-start(f32[528,256]{1,0:T(8,128)} %get-tuple-element.53), channel_id=1, source_target_pairs={{12,8},{8,4},{4,0},{13,9},{9,5},{5,1},{14,10},{10,6},{6,2},{15,11}... | collective-permute-start | bytes 1622024 | tf_op jit(solution)/shard_map/ppermute | solution.py:408
  111.7 19.3 %copy-start.2 = (f32[512,256]{1,0:T(8,128)S(1)}, f32[512,256]{1,0:T(8,128)}, u32[]{:S(2)}) copy-start(f32[512,256]{1,0:T(8,128)} %copy-done.1) | copy-start | bytes 1572868
  111.7 23.7 %collective-permute-start.10 = (f32[2,16,256]{2,1,0:T(8,128)S(1)}, f32[2,16,256]{2,1,0:T(8,128)S(1)}, u32[]{:S(2)}, u32[]{:S(2)}) collective-permute-start(f32[2,16,256]{2,1,0:T(8,128)S(1)} %gains.2), channel_id=1, source_target_pairs={{0,4},{4,8},{8,12},{12,0},{1,5},{5,9},{9,13},{13,1},{2,6},{6,10},{... | collective-permute-start | bytes 98312 | tf_op jit(solution)/shard_map/ppermute | solution.py:435
  114.4 22.0 %collective-permute-start.8 = (f32[2,16,256]{2,1,0:T(8,128)S(1)}, f32[2,16,256]{2,1,0:T(8,128)S(1)}, u32[]{:S(2)}, u32[]{:S(2)}) collective-permute-start(f32[2,16,256]{2,1,0:T(8,128)S(1)} %gains.2), channel_id=1, source_target_pairs={{0,12},{4,0},{8,4},{12,8},{1,13},{5,1},{9,5},{13,9},{2,14},{6,2},{... | collective-permute-start | bytes 98312 | tf_op jit(solution)/shard_map/ppermute | solution.py:435
  115.5 20.8 %collective-permute-start.9 = (f32[2,16,256]{2,1,0:T(8,128)S(1)}, f32[2,16,256]{2,1,0:T(8,128)S(1)}, u32[]{:S(2)}, u32[]{:S(2)}) collective-permute-start(f32[2,16,256]{2,1,0:T(8,128)S(1)} %gains.2), channel_id=1, source_target_pairs={{0,8},{4,12},{8,0},{12,4},{1,9},{5,13},{9,1},{13,5},{2,10},{6,14},... | collective-permute-start | bytes 98312 | tf_op jit(solution)/shard_map/ppermute | solution.py:435
  133.6 4.0 %collective-permute-start.18 = (f32[2,16,256]{2,1,0:T(8,128)S(1)}, f32[2,16,256]{2,1,0:T(8,128)S(1)}, u32[]{:S(2)}, u32[]{:S(2)}) collective-permute-start(f32[2,16,256]{2,1,0:T(8,128)S(1)} %gains.3), channel_id=1, source_target_pairs={{0,12},{4,0},{8,4},{12,8},{1,13},{5,1},{9,5},{13,9},{2,14},{6,2},{... | collective-permute-start | bytes 98312 | tf_op jit(solution)/shard_map/ppermute | solution.py:435
  134.6 4.8 %collective-permute-start.19 = (f32[2,16,256]{2,1,0:T(8,128)S(1)}, f32[2,16,256]{2,1,0:T(8,128)S(1)}, u32[]{:S(2)}, u32[]{:S(2)}) collective-permute-start(f32[2,16,256]{2,1,0:T(8,128)S(1)} %gains.3), channel_id=1, source_target_pairs={{0,8},{4,12},{8,0},{12,4},{1,9},{5,13},{9,1},{13,5},{2,10},{6,14},... | collective-permute-start | bytes 98312 | tf_op jit(solution)/shard_map/ppermute | solution.py:435
  135.4 5.7 %collective-permute-start.20 = (f32[2,16,256]{2,1,0:T(8,128)S(1)}, f32[2,16,256]{2,1,0:T(8,128)S(1)}, u32[]{:S(2)}, u32[]{:S(2)}) collective-permute-start(f32[2,16,256]{2,1,0:T(8,128)S(1)} %gains.3), channel_id=1, source_target_pairs={{0,4},{4,8},{8,12},{12,0},{1,5},{5,9},{9,13},{13,1},{2,6},{6,10},{... | collective-permute-start | bytes 98312 | tf_op jit(solution)/shard_map/ppermute | solution.py:435
  136.4 4.8 %collective-permute-start.11 = (f32[2,16,256]{2,1,0:T(8,128)S(1)}, f32[2,16,256]{2,1,0:T(8,128)S(1)}, u32[]{:S(2)}, u32[]{:S(2)}) collective-permute-start(f32[2,16,256]{2,1,0:T(8,128)S(1)} %select_select_fusion.2), channel_id=1, source_target_pairs={{0,1},{1,0},{2,3},{3,2},{4,5},{5,4},{6,7},{7,6},{8,9},{9,8},{10,11... | collective-permute-start | bytes 98312 | tf_op jit(solution)/shard_map/ppermute | solution.py:444
  141.1 1.3 collective-permute-start.21
  (23 other events, 136.2 us)
